TPU v7x, 512 devices: a whole 4x4x16 slice. The times are simulated.
512 devices in a mesh: prow: 64 (over z, y), pcol: 8 (over x, core).
Axes of the slice: x: 4, y: 4, z: 16, core: 2. Of those that a mesh axis runs over, the one named last changes fastest.
Arguments:
- leaf_rhs: bfloat16 [1024, 64, 256], P(('prow', 'pcol')), may hold values from -6 to 6
- leaf_inverse: bfloat16 [1024, 256, 256], P(('prow', 'pcol')), as said below
- leaf_lower: bfloat16 [1024, 12, 256, 256], P(('prow', 'pcol')), may hold values from -0.02734375 to 0.02734375
- leaf_links: int32 [1024, 12], P(('prow', 'pcol')), may hold values from 0 to 63, as said below
- sep_rhs: bfloat16 [64, 64, 256], P('prow'), may hold values from -6 to 6
- sep_inverse: bfloat16 [64, 256, 256], P('prow'), as said below
Outputs:
- leaf_solution: bfloat16 [1024, 64, 256], P(('prow', 'pcol'))
- sep_solution: bfloat16 [64, 64, 256], P('prow')
Inputs may be any that keep to these rules, and one draw needn't show every extreme that they name: `leaf_links`: leaf i lies on the device of block row p = i // 16; the 24 entries of the 2 leaves of one device (aligned blocks of 2 rows) are exactly the separators (p + d) mod 64 for d from -(12) to 10 and for d = 32, each once, in an order drawn for each device. `leaf_inverse`: lower triangular with a positive diagonal. `sep_inverse`: lower triangular with a positive diagonal.
All inputs are finite; a program needn't handle non-finite values.
Results may differ from a plain program's by a relative error of at most 0.0061.
Values may be sent and summed in bfloat16 or wider, within the bound.
No kernel may reach another device: no remote copies, remote signals or barrier semaphores. Data moves between devices by JAX's collectives and lax.ppermute only.
A program may use at most 64 MiB of HBM per device.

v0:
```python
import jax
import jax.numpy as jnp
from jax import lax
from jax.sharding import PartitionSpec as P


def separator_solve(right_side, sep_inverse):
    middle = jnp.einsum(
        "srb,sab->sra", right_side, sep_inverse, preferred_element_type=jnp.float32
    ).astype(jnp.bfloat16)
    return jnp.einsum(
        "sra,sac->src", middle, sep_inverse, preferred_element_type=jnp.float32
    ).astype(jnp.bfloat16)


def shards(leaf_rhs, leaf_inverse, leaf_lower, leaf_links, sep_rhs, sep_inverse):
    leaf_count = leaf_rhs.shape[0]
    rhs_count = leaf_rhs.shape[1]
    block_width = leaf_rhs.shape[2]
    link_count = leaf_links.shape[1]
    seps_all = sep_rhs.shape[0] * lax.axis_size("prow")
    forward = jnp.einsum(
        "lrb,lab->lra", leaf_rhs, leaf_inverse, preferred_element_type=jnp.float32
    ).astype(jnp.bfloat16)
    link_terms = jnp.einsum(
        "lkab,lrb->lkra", leaf_lower, forward, preferred_element_type=jnp.float32
    )
    flat_links = leaf_links.reshape(-1)
    spread = jnp.zeros((seps_all, rhs_count, block_width), jnp.float32)
    spread = spread.at[flat_links].add(link_terms.reshape(-1, rhs_count, block_width))
    partial_rows = lax.psum_scatter(spread, "prow", scatter_dimension=0, tiled=True)
    sep_sums = lax.psum(partial_rows, "pcol")
    right_side = (sep_rhs.astype(jnp.float32) - sep_sums).astype(jnp.bfloat16)
    sep_solution = separator_solve(right_side, sep_inverse)
    every_sep = lax.all_gather(sep_solution, "prow", axis=0, tiled=True)
    picked = every_sep[flat_links].reshape(leaf_count, link_count, rhs_count, block_width)
    back_terms = jnp.einsum(
        "lkab,lkra->lrb", leaf_lower, picked, preferred_element_type=jnp.float32
    )
    remainder = (forward.astype(jnp.float32) - back_terms).astype(jnp.bfloat16)
    leaf_solution = jnp.einsum(
        "lrb,lbc->lrc", remainder, leaf_inverse, preferred_element_type=jnp.float32
    ).astype(jnp.bfloat16)
    return (leaf_solution, sep_solution)


def solution(mesh):
    placed = (
        P(("prow", "pcol"), None, None),
        P(("prow", "pcol"), None, None),
        P(("prow", "pcol"), None, None, None),
        P(("prow", "pcol"), None),
        P("prow", None, None),
        P("prow", None, None),
    )
    return jax.shard_map(
        shards,
        mesh=mesh,
        in_specs=placed,
        out_specs=(P(("prow", "pcol"), None, None), P("prow", None, None)),
        check_vma=False,
    )
```

profile of v0, /device:TPU:1, one launch (start us, length us, event | category | flops | bytes accessed | tf_op | source)
XLA Modules:
  0.0 946.8 jit_solution(11752235461715104014)
XLA Ops:
  7.2 0.0 copy-start
  7.2 0.0 reduce-scatter.2.cloned.1.call-start
  7.2 0.9 reshape.54
  8.1 1.2 convolution_convert_fusion.1
  9.3 0.0 copy-done
  9.3 2.3 fusion.5
  11.6 2.5 broadcast_in_dim.2
  14.1 6.7 scatter_fusion
  20.8 0.0 copy-start.2
  20.8 0.0 copy-start.1
  20.8 0.0 reduce-scatter.2.cloned.1.call-update
  20.8 0.0 all-reduce.2.cloned.1.call-start
  20.9 694.3 %reduce-scatter.2.cloned.1.call-done = f32[1,64,256]{2,1,0:T(8,128)} async-done(((f32[64,64,256]{2,1,0:T(8,128)}), f32[1,64,256]{2,1,0:T(8,128)}) %reduce-scatter.2.cloned.1.call-update) | async-done | bytes 65552 | tf_op jit(solution)/shard_map/reduce_scatter | solution.py:31
  715.1 0.0 all-reduce.2.cloned.1.call-update
  715.2 0.0 all-gather.3.cloned.1.call-start
  715.2 83.3 %all-reduce.2.cloned.1.call-done = f32[1,64,256]{2,1,0:T(8,128)} async-done(((f32[1,64,256]{2,1,0:T(8,128)}), f32[1,64,256]{2,1,0:T(8,128)}) %all-reduce.2.cloned.1.call-update) | async-done | bytes 65552 | tf_op jit(solution)/shard_map/psum | solution.py:32
  798.5 0.0 copy-done.2
  798.5 1.9 convolution_convert_fusion.2
  800.4 0.0 all-gather.3.cloned.1.call-update
  800.4 134.1 %all-gather.3.cloned.1.call-done = bf16[4096,256]{1,0:T(8,128)(2,1)} async-done(((bf16[64,256]{1,0:T(8,128)(2,1)}), bf16[4096,256]{1,0:T(8,128)(2,1)}) %all-gather.3.cloned.1.call-update) | async-done | bytes 2097168 | tf_op jit(solution)/shard_map/all_gather | solution.py:35
  934.6 3.1 gather_fusion
  937.7 0.0 copy-done.1
  937.7 2.6 convolution_convert_fusion
  (2 shorter events, 0.0 us)
Async XLA Ops:
  7.2 2.2 copy-start
  7.2 708.0 %reduce-scatter.2.cloned.1.call-start = ((), (), s32[]{:S(2)}) async-start(), calls=%async_computation.1 | async-start | bytes 4259840 | tf_op jit(solution)/shard_map/reduce_scatter | solution.py:31
  20.8 777.7 %copy-start.2 = (bf16[1,64,256]{2,1,0:T(8,128)(2,1)S(1)}, bf16[1,64,256]{2,1,0:T(8,128)(2,1)}, u32[]{:S(2)}) copy-start(bf16[1,64,256]{2,1,0:T(8,128)(2,1)} %param.10) | copy-start | bytes 98308
  20.8 916.9 %copy-start.1 = (bf16[2,256,256]{2,1,0:T(8,128)(2,1)S(1)}, bf16[2,256,256]{2,1,0:T(8,128)(2,1)}, u32[]{:S(2)}) copy-start(bf16[2,256,256]{2,1,0:T(8,128)(2,1)} %param.7) | copy-start | bytes 786436
  20.8 777.7 %all-reduce.2.cloned.1.call-start = ((), (), s32[]{:S(2)}) async-start(), calls=%async_computation.2 | async-start | bytes 131072 | tf_op jit(solution)/shard_map/psum | solution.py:32
  715.2 219.4 %all-gather.3.cloned.1.call-start = ((), (), s32[]{:S(2)}) async-start(), calls=%async_computation.3 | async-start | bytes 2129920 | tf_op jit(solution)/shard_map/all_gather | solution.py:35
Sparse Core Ops, SparseCore 0:
  20.9 694.1 reduce-scatter.1
  717.5 80.8 all-reduce.1
  802.0 132.5 all-gather.2
where the time goes:
time: 955 us; the launch traced here: 947 us
  waiting for transfers between devices  912 us (95%)
  between operations  13.8 us (1%)
    reduce_scatter x1, waiting for transfers between devices, shards(): lax.psum_scatter(spread, 'prow', scatter_dimension=0, tiled=True)  694 us
    all_gather x1, waiting for transfers between devices, shards(): every_sep = lax.all_gather(sep_solution, 'prow', axis=0, tiled=True)  134 us
    psum x1, waiting for transfers between devices, shards(): sep_sums = lax.psum(partial_rows, 'pcol')  83.3 us
  transfers between devices with their start and end apart: 3, of which 3 were waited for; matrix products, arithmetic and copies ran while one was open for 0% of the time, Pallas kernels for 0%

commit v1 on v0

v1 whole, which is shorter than its diff:
```python
import jax
import jax.numpy as jnp
from jax import lax
from jax.experimental import pallas as pl
from jax.experimental.pallas import tpu as pltpu
from jax.sharding import Mesh
from jax.sharding import PartitionSpec as P

NZ, NY, NX, NC = 16, 4, 4, 2
FACE = ("y", "x")
NFACE = NY * NX
REACH = 3
NSLOT = 8
R, B = 64, 256
RP = R // (NX * NC)
LANES = 128
CHUNKS = 8

F32, BF16 = jnp.float32, jnp.bfloat16
SMEM = pl.BlockSpec(memory_space=pltpu.SMEM)
VMEM = pl.BlockSpec(memory_space=pltpu.VMEM)
HBM = pl.BlockSpec(memory_space=pltpu.HBM)
PARAMS = pltpu.CompilerParams(vmem_limit_bytes=32 * 1024 * 1024)


def dot_nt(a, b):
    return lax.dot_general(a, b, (((1,), (1,)), ((), ())), preferred_element_type=F32)


def dot_nn(a, b):
    return lax.dot_general(a, b, (((1,), (0,)), ((), ())), preferred_element_type=F32)


def slot_of(link, z):
    plane_slot = jnp.minimum((link // NY - z + REACH + NZ) % NZ, NSLOT - 1)
    return (link % NY) * NSLOT + plane_slot


def plane_of(slot, z):
    return (z + (NZ // 2 if slot == NSLOT - 1 else slot - REACH) + NZ) % NZ


def rows_of(x, c):
    return pl.ds(pl.multiple_of((x * NC + c) * RP, RP), RP)


def fold(rows):
    return jnp.concatenate([rows[:, :LANES], rows[:, LANES:]], axis=0).astype(BF16)


def unfold(tile):
    tile = tile.astype(F32)
    return jnp.concatenate([tile[:RP], tile[RP:]], axis=1)


def link_kernel(at_ref, links_ref, rhs_ref, inverse_ref, lower_hbm, forward_ref, keep_ref, send_ref, lower_ref, terms_ref, sems):
    leaves, links = links_ref.shape
    per = leaves * links // CHUNKS
    copies = [
        pltpu.make_async_copy(lower_hbm.at[pl.ds(n * per, per)], lower_ref.at[pl.ds(n * per, per)], sems.at[n])
        for n in range(CHUNKS)
    ]
    for copy in copies:
        copy.start()
    z, c = at_ref[0], at_ref[3]
    terms_ref[...] = jnp.zeros_like(terms_ref)
    for i in range(leaves):
        forward = dot_nt(rhs_ref[i], inverse_ref[i]).astype(BF16)
        forward_ref[i] = forward
        for k in range(links):
            n = i * links + k
            if n % per == 0:
                copies[n // per].wait()
            terms_ref[slot_of(links_ref[i, k], z)] = dot_nt(forward, lower_ref[n])
    for y in range(NY):
        for x in range(NX):
            mine = terms_ref[y * NSLOT:(y + 1) * NSLOT, rows_of(x, c), :]
            keep_ref[y * NX + x] = mine.reshape(NSLOT * RP, B)
            other = terms_ref[y * NSLOT:(y + 1) * NSLOT, rows_of(x, 1 - c), :]
            send_ref[y * NX + x] = other.reshape(NSLOT * RP, B).astype(BF16)


def pair_kernel(keep_ref, part_ref, out_ref):
    out_ref[...] = (keep_ref[...] + part_ref[...].astype(F32)).astype(BF16)


def face_kernel(at_ref, parts_ref, out_ref):
    z = at_ref[0]
    total = parts_ref[0].astype(F32)
    for n in range(1, NFACE):
        total = total + parts_ref[n].astype(F32)
    out_ref[...] = jnp.zeros_like(out_ref)
    for slot in range(NSLOT):
        out_ref[plane_of(slot, z)] = fold(total[slot * RP:(slot + 1) * RP])


def solve_kernel(at_ref, parts_ref, rhs_ref, inverse_ref, out_ref, rhs32_ref):
    rhs32_ref[...] = rhs_ref[0].astype(F32)
    sums = parts_ref[0].astype(F32)
    for n in range(1, NZ):
        sums = sums + parts_ref[n].astype(F32)
    sums = jnp.concatenate([sums[:RP], sums[RP:]], axis=1)
    right_side = (rhs32_ref[rows_of(at_ref[2], at_ref[3]), :] - sums).astype(BF16)
    middle = dot_nt(right_side, inverse_ref[0]).astype(BF16)
    solved = dot_nn(middle, inverse_ref[0])
    out_ref[...] = jnp.broadcast_to(fold(solved)[None], out_ref.shape)


def pick_kernel(at_ref, planes_ref, out_ref):
    z = at_ref[0]
    picked = jnp.concatenate([unfold(planes_ref[plane_of(slot, z)]) for slot in range(NSLOT)], axis=0)
    out_ref[...] = jnp.broadcast_to(picked.astype(BF16)[None], out_ref.shape)


def back_kernel(at_ref, links_ref, mine_ref, other_ref, lower_ref, forward_ref, inverse_ref, leaf_ref, sep_ref, seps_ref, rows_ref):
    z, row, c = at_ref[0], at_ref[1], at_ref[3]
    leaves, links = links_ref.shape
    for y in range(NY):
        for x in range(NX):
            mine = mine_ref[y * NX + x].astype(F32).reshape(NSLOT, RP, B)
            seps_ref[y * NSLOT:(y + 1) * NSLOT, rows_of(x, c), :] = mine
            other = other_ref[y * NX + x].astype(F32).reshape(NSLOT, RP, B)
            seps_ref[y * NSLOT:(y + 1) * NSLOT, rows_of(x, 1 - c), :] = other
    sep_ref[0] = seps_ref[row * NSLOT + REACH].astype(BF16)
    for i in range(leaves):
        for k in range(links):
            rows_ref[:, k * B:(k + 1) * B] = seps_ref[slot_of(links_ref[i, k], z)].astype(BF16)
        back_terms = dot_nn(rows_ref[...], lower_ref[i])
        remainder = (forward_ref[i].astype(F32) - back_terms).astype(BF16)
        leaf_ref[i] = dot_nn(remainder, inverse_ref[i]).astype(BF16)


def call(kernel, outs, in_specs, scratch=()):
    many = isinstance(outs, tuple)
    return pl.pallas_call(
        kernel,
        out_shape=outs,
        in_specs=in_specs,
        out_specs=tuple(VMEM for _ in outs) if many else VMEM,
        scratch_shapes=scratch,
        compiler_params=PARAMS,
    )


def shards(leaf_rhs, leaf_inverse, leaf_lower, leaf_links, sep_rhs, sep_inverse):
    leaves, links = leaf_links.shape
    at = jnp.stack([lax.axis_index(a) for a in ("z", "y", "x", "c")]).astype(jnp.int32)
    shape = jax.ShapeDtypeStruct
    swap = [(0, 1), (1, 0)]
    face = (NFACE, NSLOT * RP, B)
    column = (NZ, 2 * RP, LANES)
    forward, keep, send = call(
        link_kernel,
        (shape((leaves, R, B), BF16), shape(face, F32), shape(face, BF16)),
        [SMEM, SMEM, VMEM, VMEM, HBM],
        (
            pltpu.VMEM((leaves * links, B, B), BF16),
            pltpu.VMEM((NY * NSLOT, R, B), F32),
            pltpu.SemaphoreType.DMA((CHUNKS,)),
        ),
    )(at, leaf_links, leaf_rhs, leaf_inverse, leaf_lower.reshape(leaves * links, B, B))
    part = lax.ppermute(send, "c", swap)
    pairs = call(pair_kernel, shape(face, BF16), [VMEM, VMEM])(keep, part)
    parts = lax.all_to_all(pairs, FACE, 0, 0, tiled=True)
    sums = call(face_kernel, shape(column, BF16), [SMEM, VMEM])(at, parts)
    parts = lax.all_to_all(sums, "z", 0, 0, tiled=True)
    solved = call(
        solve_kernel, shape(column, BF16), [SMEM, VMEM, VMEM, VMEM], (pltpu.VMEM((R, B), F32),)
    )(at, parts, sep_rhs, sep_inverse)
    planes = lax.all_to_all(solved, "z", 0, 0, tiled=True)
    picked = call(pick_kernel, shape(face, BF16), [SMEM, VMEM])(at, planes)
    mine = lax.all_to_all(picked, FACE, 0, 0, tiled=True)
    other = lax.ppermute(mine, "c", swap)
    return call(
        back_kernel,
        (shape((leaves, R, B), BF16), shape((1, R, B), BF16)),
        [SMEM, SMEM] + [VMEM] * 5,
        (pltpu.VMEM((NY * NSLOT, R, B), F32), pltpu.VMEM((R, links * B), BF16)),
    )(at, leaf_links, mine, other, leaf_lower.reshape(leaves, links * B, B), forward, leaf_inverse)


def solution(mesh):
    grid = Mesh(mesh.devices.reshape(NZ, NY, NX, NC), ("z", "y", "x", "c"))
    every, row = ("z", "y", "x", "c"), ("z", "y")
    return jax.shard_map(
        shards,
        mesh=grid,
        in_specs=(P(every), P(every), P(every), P(every), P(row), P(row)),
        out_specs=(P(every), P(row)),
        check_vma=False,
    )
```

time: 955 us -> 99.1 us (0.10)
  waiting for transfers between devices: 912 us -> 3.03 us
  blocking collectives: 0 us -> 65 us
  starting transfers between devices: 0.12 us -> 16.2 us
  between operations: 13.8 us -> 0.7 us
    reduce_scatter x1 -> x0, waiting for transfers between devices: 694 us -> none  [shards(): lax.psum_scatter(spread, 'prow', scatter_dimension=0, tiled=True)]
    all_gather x1 -> x0, waiting for transfers between devices: 134 us -> none  [shards(): every_sep = lax.all_gather(sep_solution, 'prow', axis=0, tiled=True)]
    psum x1 -> x0, waiting for transfers between devices: 83.3 us -> none  [shards(): sep_sums = lax.psum(partial_rows, 'pcol')]
    all_to_all x0 -> x4, blocking collectives: none -> 65 us  [the longest x1 24.6 us: shards(): parts = lax.all_to_all(sums, 'z', 0, 0, tiled=True)]
    ppermute x0 -> x2, starting transfers between devices: none -> 16.2 us  [the longest x1 9.05 us: shards(): part = lax.ppermute(send, 'c', swap)]
  transfers between devices with their start and end apart: 3 -> 2, of which waited for: 3 -> 2; matrix products, arithmetic and copies ran while one was open for 0% -> 0% of each run, Pallas kernels for 0% -> 0%
where the time goes in v1:
time: 99.1 us; the launch traced here: 98.7 us
  blocking collectives  65 us (66%)
  starting transfers between devices  16.2 us (16%)
  Pallas kernels  9.32 us (9%)
  local copies, waits for them, and re-layouts  4.38 us (4%)
  waiting for transfers between devices  3.03 us (3%)
    all_to_all x1, blocking collectives, shards(): parts = lax.all_to_all(sums, 'z', 0, 0, tiled=True)  24.6 us
    all_to_all x1, blocking collectives, shards(): planes = lax.all_to_all(solved, 'z', 0, 0, tiled=True)  14.4 us
    all_to_all x1, blocking collectives, shards(): parts = lax.all_to_all(pairs, FACE, 0, 0, tiled=True)  13.6 us
    all_to_all x1, blocking collectives, shards(): mine = lax.all_to_all(picked, FACE, 0, 0, tiled=True)  12.4 us
    ppermute x1, starting transfers between devices, shards(): part = lax.ppermute(send, 'c', swap)  9.05 us
    ppermute x1, starting transfers between devices, shards(): other = lax.ppermute(mine, 'c', swap)  7.17 us
    pallas_call x1, Pallas kernels, shards(): call(link_kernel, (shape((leaves, R, B), BF16), shape(face, F32), shape(f...  4.66 us
    unnamed x16, local copies, waits for them, and re-layouts  4.38 us
  transfers between devices with their start and end apart: 2, of which 2 were waited for; matrix products, arithmetic and copies ran while one was open for 0% of the time, Pallas kernels for 0%

profile of v1, /device:TPU:1, one launch (start us, length us, event | category | flops | bytes accessed | tf_op | source)
XLA Modules:
  0.0 98.7 jit_solution(1318170937156475447)
XLA Ops:
  0.6 0.1 pad_add_fusion.at_ref
  0.7 1.9 %copy-done = bf16[2,12,256,256]{3,2,1,0:T(8,128)(2,1)S(1)} copy-done((bf16[2,12,256,256]{3,2,1,0:T(8,128)(2,1)S(1)}, bf16[2,12,256,256]{3,2,1,0:T(8,128)(2,1)}, u32[]{:S(2)}) %copy-start) | copy-done | bytes 3145752
  2.6 0.9 copy-done.2
  3.6 0.8 copy-done.5
  4.4 0.7 copy-done.7
  5.1 4.7 %shard_map.77 = (bf16[2,64,256]{2,1,0:T(8,128)(2,1)S(1)}, f32[16,64,256]{2,1,0:T(8,128)S(1)}, bf16[16,64,256]{2,1,0:T(8,128)(2,1)S(1)}) custom-call(s32[4]{0:T(128)S(1)} %pad_add_fusion.at_ref, s32[2,12]{1,0:T(2,128)S(1)} %copy-done.7, bf16[2,64,256]{2,1,0:T(8,128)(2,1)S(1)} %copy-done.5, bf16[2,256,256]{2,1,0:T(8,128)(2,1)S(1)} %copy-done.2, ...), custom_call_target="tpu_custom_call" | custom-call | tf_op jit(solution)/shard_map/pallas_call | solution.py:152
  9.7 0.0 copy-start.1
  9.8 0.0 copy-start.3
  9.8 9.0 %collective-permute-start = (bf16[16,64,256]{2,1,0:T(8,128)(2,1)S(1)}, bf16[16,64,256]{2,1,0:T(8,128)(2,1)S(1)}, u32[]{:S(2)}, u32[]{:S(2)}) collective-permute-start(bf16[16,64,256]{2,1,0:T(8,128)(2,1)S(1)} %get-tuple-element.6), channel_id=1, source_target_pairs={{0,1},{1,0},{2,3},{3,2},{4,5},{5,4},{6,7},{7,6},{8,9},{9,8},{10,11... | collective-permute-start | bytes 1572872 | tf_op jit(solution)/shard_map/ppermute | solution.py:162
  18.8 1.5 %collective-permute-done.part_ref = bf16[16,64,256]{2,1,0:T(8,128)(2,1)S(1)} collective-permute-done((bf16[16,64,256]{2,1,0:T(8,128)(2,1)S(1)}, bf16[16,64,256]{2,1,0:T(8,128)(2,1)S(1)}, u32[]{:S(2)}, u32[]{:S(2)}) %collective-permute-start) | collective-permute-done | bytes 524320 | tf_op jit(solution)/shard_map/ppermute | solution.py:162
  20.3 0.1 shard_map.78
  20.4 13.6 %all_to_all.20.parts_ref = bf16[16,64,256]{2,1,0:T(8,128)(2,1)S(1)} all-to-all(bf16[16,64,256]{2,1,0:T(8,128)(2,1)S(1)} %shard_map.78), channel_id=1, replica_groups=mesh['z'=16,'y'=4,'x'=4,'c'=2] {'y','x'}, dimensions={0} | all-to-all | bytes 1048576 | tf_op jit(solution)/shard_map/all_to_all | solution.py:164
  34.0 0.6 shard_map.79
  34.7 24.6 %all_to_all.21.parts_ref = bf16[16,16,128]{2,1,0:T(8,128)(2,1)S(1)} all-to-all(bf16[16,16,128]{2,1,0:T(8,128)(2,1)S(1)} %shard_map.79), channel_id=1, replica_groups=mesh['z'=16,'y'=4,'x'=4,'c'=2] {'z'}, dimensions={0} | all-to-all | bytes 131072 | tf_op jit(solution)/shard_map/all_to_all | solution.py:166
  59.2 0.0 copy-done.4
  59.2 0.0 copy-done.6
  59.2 0.8 shard_map.80
  60.1 14.4 %all_to_all.22.planes_ref = bf16[16,16,128]{2,1,0:T(8,128)(2,1)S(1)} all-to-all(bf16[16,16,128]{2,1,0:T(8,128)(2,1)S(1)} %shard_map.80), channel_id=1, replica_groups=mesh['z'=16,'y'=4,'x'=4,'c'=2] {'z'}, dimensions={0} | all-to-all | bytes 131072 | tf_op jit(solution)/shard_map/all_to_all | solution.py:170
  74.5 0.6 shard_map.81
  75.1 12.4 %all_to_all.23.mine_ref = bf16[16,64,256]{2,1,0:T(8,128)(2,1)S(1)} all-to-all(bf16[16,64,256]{2,1,0:T(8,128)(2,1)S(1)} %shard_map.81), channel_id=1, replica_groups=mesh['z'=16,'y'=4,'x'=4,'c'=2] {'y','x'}, dimensions={0} | all-to-all | bytes 1048576 | tf_op jit(solution)/shard_map/all_to_all | solution.py:172
  87.4 7.2 %collective-permute-start.1 = (bf16[16,64,256]{2,1,0:T(8,128)(2,1)S(1)}, bf16[16,64,256]{2,1,0:T(8,128)(2,1)S(1)}, u32[]{:S(2)}, u32[]{:S(2)}) collective-permute-start(bf16[16,64,256]{2,1,0:T(8,128)(2,1)S(1)} %all_to_all.23.mine_ref), channel_id=1, source_target_pairs={{0,1},{1,0},{2,3},{3,2},{4,5},{5,4},{6,7},{7,6},{8,9},{9,8},{10,11... | collective-permute-start | bytes 1572872 | tf_op jit(solution)/shard_map/ppermute | solution.py:173
  94.6 1.5 %collective-permute-done.1.other_ref = bf16[16,64,256]{2,1,0:T(8,128)(2,1)S(1)} collective-permute-done((bf16[16,64,256]{2,1,0:T(8,128)(2,1)S(1)}, bf16[16,64,256]{2,1,0:T(8,128)(2,1)S(1)}, u32[]{:S(2)}, u32[]{:S(2)}) %collective-permute-start.1) | collective-permute-done | bytes 524320 | tf_op jit(solution)/shard_map/ppermute | solution.py:173
  96.1 0.0 copy-done.1
  96.1 2.6 %shard_map.82 = (bf16[2,64,256]{2,1,0:T(8,128)(2,1)}, bf16[1,64,256]{2,1,0:T(8,128)(2,1)}) custom-call(s32[4]{0:T(128)S(1)} %pad_add_fusion.at_ref, s32[2,12]{1,0:T(2,128)S(1)} %copy-done.7, bf16[16,64,256]{2,1,0:T(8,128)(2,1)S(1)} %all_to_all.23.mine_ref, bf16[16,64,256]{2,1,0:T(8,128)(2,1)S(1)} %collective-permute-done.1.other_ref, ...), custom_call_target="tpu_custom_call" | custom-call | tf_op jit(solution)/shard_map/pallas_call | solution.py:174
  (7 shorter events, 0.0 us)
Async XLA Ops:
  0.7 1.9 %copy-start = (bf16[2,12,256,256]{3,2,1,0:T(8,128)(2,1)S(1)}, bf16[2,12,256,256]{3,2,1,0:T(8,128)(2,1)}, u32[]{:S(2)}) copy-start(bf16[2,12,256,256]{3,2,1,0:T(8,128)(2,1)} %param.8) | copy-start | bytes 9437188
  2.6 0.9 copy-start.2
  3.6 0.8 copy-start.5
  4.4 0.7 copy-start.7
  5.1 54.2 %copy-start.4 = (bf16[1,256,256]{2,1,0:T(8,128)(2,1)S(1)}, bf16[1,256,256]{2,1,0:T(8,128)(2,1)}, u32[]{:S(2)}) copy-start(bf16[1,256,256]{2,1,0:T(8,128)(2,1)} %inverse_ref.4) | copy-start | bytes 393220
  5.1 54.2 %copy-start.6 = (bf16[1,64,256]{2,1,0:T(8,128)(2,1)S(1)}, bf16[1,64,256]{2,1,0:T(8,128)(2,1)}, u32[]{:S(2)}) copy-start(bf16[1,64,256]{2,1,0:T(8,128)(2,1)} %rhs_ref.3) | copy-start | bytes 98308
  9.7 86.4 %copy-start.1 = (bf16[2,12,256,256]{3,2,1,0:T(8,128)(2,1)S(1)}, bf16[2,12,256,256]{3,2,1,0:T(8,128)(2,1)}, u32[]{:S(2)}) copy-start(bf16[2,12,256,256]{3,2,1,0:T(8,128)(2,1)} %param.8) | copy-start | bytes 9437188
  9.8 86.4 %copy-start.3 = (bf16[2,256,256]{2,1,0:T(8,128)(2,1)S(1)}, bf16[2,256,256]{2,1,0:T(8,128)(2,1)}, u32[]{:S(2)}) copy-start(bf16[2,256,256]{2,1,0:T(8,128)(2,1)} %inverse_ref.5) | copy-start | bytes 786436
  9.8 10.6 %collective-permute-start = (bf16[16,64,256]{2,1,0:T(8,128)(2,1)S(1)}, bf16[16,64,256]{2,1,0:T(8,128)(2,1)S(1)}, u32[]{:S(2)}, u32[]{:S(2)}) collective-permute-start(bf16[16,64,256]{2,1,0:T(8,128)(2,1)S(1)} %get-tuple-element.6), channel_id=1, source_target_pairs={{0,1},{1,0},{2,3},{3,2},{4,5},{5,4},{6,7},{7,6},{8,9},{9,8},{10,11... | collective-permute-start | bytes 1572872 | tf_op jit(solution)/shard_map/ppermute | solution.py:162
  87.4 8.7 %collective-permute-start.1 = (bf16[16,64,256]{2,1,0:T(8,128)(2,1)S(1)}, bf16[16,64,256]{2,1,0:T(8,128)(2,1)S(1)}, u32[]{:S(2)}, u32[]{:S(2)}) collective-permute-start(bf16[16,64,256]{2,1,0:T(8,128)(2,1)S(1)} %all_to_all.23.mine_ref), channel_id=1, source_target_pairs={{0,1},{1,0},{2,3},{3,2},{4,5},{5,4},{6,7},{7,6},{8,9},{9,8},{10,11... | collective-permute-start | bytes 1572872 | tf_op jit(solution)/shard_map/ppermute | solution.py:173

commit v2 on v1

--- a/solution.py
+++ b/solution.py
@@ -13,6 +13,7 @@
 NSLOT = 8
 R, B = 64, 256
 RP = R // (NX * NC)
+RH = R // NC
 LANES = 128
 CHUNKS = 8
 
@@ -41,7 +42,7 @@
 
 
 def rows_of(x, c):
-    return pl.ds(pl.multiple_of((x * NC + c) * RP, RP), RP)
+    return pl.ds(pl.multiple_of((c * NX + x) * RP, RP), RP)
 
 
 def fold(rows):
@@ -53,24 +54,33 @@
     return jnp.concatenate([tile[:RP], tile[RP:]], axis=1)
 
 
-def link_kernel(at_ref, links_ref, rhs_ref, inverse_ref, lower_hbm, forward_ref, keep_ref, send_ref, lower_ref, terms_ref, sems):
+def link_kernel(at_ref, links_hbm, rhs_hbm, inverse_hbm, lower_hbm, forward_ref, keep_ref, send_ref,
+                links_ref, rhs_ref, inverse_ref, lower_ref, terms_ref, sems):
     leaves, links = links_ref.shape
     per = leaves * links // CHUNKS
     copies = [
+        pltpu.make_async_copy(links_hbm, links_ref, sems.at[CHUNKS]),
+        pltpu.make_async_copy(rhs_hbm, rhs_ref, sems.at[CHUNKS + 1]),
+        pltpu.make_async_copy(inverse_hbm, inverse_ref, sems.at[CHUNKS + 2]),
+    ] + [
         pltpu.make_async_copy(lower_hbm.at[pl.ds(n * per, per)], lower_ref.at[pl.ds(n * per, per)], sems.at[n])
         for n in range(CHUNKS)
     ]
     for copy in copies:
         copy.start()
+    small, blocks = copies[:3], copies[3:]
     z, c = at_ref[0], at_ref[3]
     terms_ref[...] = jnp.zeros_like(terms_ref)
+    for copy in small:
+        copy.wait()
     for i in range(leaves):
-        forward = dot_nt(rhs_ref[i], inverse_ref[i]).astype(BF16)
-        forward_ref[i] = forward
+        forward_ref[i] = dot_nt(rhs_ref[i], inverse_ref[i]).astype(BF16).reshape(NC, RH, B)
+    for i in range(leaves):
+        forward = forward_ref[i].reshape(R, B)
         for k in range(links):
             n = i * links + k
             if n % per == 0:
-                copies[n // per].wait()
+                blocks[n // per].wait()
             terms_ref[slot_of(links_ref[i, k], z)] = dot_nt(forward, lower_ref[n])
     for y in range(NY):
         for x in range(NX):
@@ -112,22 +122,44 @@
     out_ref[...] = jnp.broadcast_to(picked.astype(BF16)[None], out_ref.shape)
 
 
-def back_kernel(at_ref, links_ref, mine_ref, other_ref, lower_ref, forward_ref, inverse_ref, leaf_ref, sep_ref, seps_ref, rows_ref):
-    z, row, c = at_ref[0], at_ref[1], at_ref[3]
+def back_half(z, row, links_ref, parts_ref, lower_ref, forward_ref, inverse_ref, seps_ref, rows_ref, half):
     leaves, links = links_ref.shape
     for y in range(NY):
         for x in range(NX):
-            mine = mine_ref[y * NX + x].astype(F32).reshape(NSLOT, RP, B)
-            seps_ref[y * NSLOT:(y + 1) * NSLOT, rows_of(x, c), :] = mine
-            other = other_ref[y * NX + x].astype(F32).reshape(NSLOT, RP, B)
-            seps_ref[y * NSLOT:(y + 1) * NSLOT, rows_of(x, 1 - c), :] = other
-    sep_ref[0] = seps_ref[row * NSLOT + REACH].astype(BF16)
+            part = parts_ref[y * NX + x].astype(F32).reshape(NSLOT, RP, B)
+            seps_ref[y * NSLOT:(y + 1) * NSLOT, x * RP:(x + 1) * RP, :] = part
+    solved = []
     for i in range(leaves):
         for k in range(links):
             rows_ref[:, k * B:(k + 1) * B] = seps_ref[slot_of(links_ref[i, k], z)].astype(BF16)
         back_terms = dot_nn(rows_ref[...], lower_ref[i])
-        remainder = (forward_ref[i].astype(F32) - back_terms).astype(BF16)
-        leaf_ref[i] = dot_nn(remainder, inverse_ref[i]).astype(BF16)
+        remainder = (forward_ref[i, half].astype(F32) - back_terms).astype(BF16)
+        solved.append(dot_nn(remainder, inverse_ref[i]).astype(BF16))
+    return solved, seps_ref[row * NSLOT + REACH].astype(BF16)
+
+
+def mine_kernel(at_ref, links_ref, parts_ref, lower_ref, forward_ref, inverse_ref, leaf_ref, sep_ref, seps_ref, rows_ref):
+    solved, sep = back_half(at_ref[0], at_ref[1], links_ref, parts_ref, lower_ref, forward_ref, inverse_ref,
+                            seps_ref, rows_ref, at_ref[3])
+    for i, rows in enumerate(solved):
+        leaf_ref[i] = rows
+    sep_ref[...] = sep
+
+
+def other_kernel(at_ref, links_ref, parts_ref, lower_ref, forward_ref, inverse_ref, leaf_half_ref, sep_half_ref,
+                 leaf_ref, sep_ref, seps_ref, rows_ref):
+    c = at_ref[3]
+    solved, sep = back_half(at_ref[0], at_ref[1], links_ref, parts_ref, lower_ref, forward_ref, inverse_ref,
+                            seps_ref, rows_ref, 1 - c)
+    for i, rows in enumerate(solved):
+        leaf_ref[i, c] = leaf_half_ref[i]
+        leaf_ref[i, 1 - c] = rows
+    sep_ref[0, c] = sep_half_ref[...]
+    sep_ref[0, 1 - c] = sep
+
+
+def stay(array):
+    return pltpu.with_memory_space_constraint(array, pltpu.HBM)
 
 
 def call(kernel, outs, in_specs, scratch=()):
@@ -151,14 +183,17 @@
     column = (NZ, 2 * RP, LANES)
     forward, keep, send = call(
         link_kernel,
-        (shape((leaves, R, B), BF16), shape(face, F32), shape(face, BF16)),
-        [SMEM, SMEM, VMEM, VMEM, HBM],
+        (shape((leaves, NC, RH, B), BF16), shape(face, F32), shape(face, BF16)),
+        [SMEM, HBM, HBM, HBM, HBM],
         (
+            pltpu.SMEM((leaves, links), jnp.int32),
+            pltpu.VMEM((leaves, R, B), BF16),
+            pltpu.VMEM((leaves, B, B), BF16),
             pltpu.VMEM((leaves * links, B, B), BF16),
             pltpu.VMEM((NY * NSLOT, R, B), F32),
-            pltpu.SemaphoreType.DMA((CHUNKS,)),
+            pltpu.SemaphoreType.DMA((CHUNKS + 3,)),
         ),
-    )(at, leaf_links, leaf_rhs, leaf_inverse, leaf_lower.reshape(leaves * links, B, B))
+    )(at, *map(stay, (leaf_links, leaf_rhs, leaf_inverse, leaf_lower.reshape(leaves * links, B, B))))
     part = lax.ppermute(send, "c", swap)
     pairs = call(pair_kernel, shape(face, BF16), [VMEM, VMEM])(keep, part)
     parts = lax.all_to_all(pairs, FACE, 0, 0, tiled=True)
@@ -171,12 +206,18 @@
     picked = call(pick_kernel, shape(face, BF16), [SMEM, VMEM])(at, planes)
     mine = lax.all_to_all(picked, FACE, 0, 0, tiled=True)
     other = lax.ppermute(mine, "c", swap)
-    return call(
-        back_kernel,
-        (shape((leaves, R, B), BF16), shape((1, R, B), BF16)),
-        [SMEM, SMEM] + [VMEM] * 5,
-        (pltpu.VMEM((NY * NSLOT, R, B), F32), pltpu.VMEM((R, links * B), BF16)),
-    )(at, leaf_links, mine, other, leaf_lower.reshape(leaves, links * B, B), forward, leaf_inverse)
+    lower = leaf_lower.reshape(leaves, links * B, B)
+    scratch = (pltpu.VMEM((NY * NSLOT, RH, B), F32), pltpu.VMEM((RH, links * B), BF16))
+    halves = call(
+        mine_kernel, (shape((leaves, RH, B), BF16), shape((RH, B), BF16)), [SMEM, SMEM] + [VMEM] * 4, scratch
+    )(at, leaf_links, mine, lower, forward, leaf_inverse)
+    leaf_solution, sep_solution = call(
+        other_kernel,
+        (shape((leaves, NC, RH, B), BF16), shape((1, NC, RH, B), BF16)),
+        [SMEM, SMEM] + [VMEM] * 6,
+        scratch,
+    )(at, leaf_links, other, lower, forward, leaf_inverse, *halves)
+    return leaf_solution.reshape(leaves, R, B), sep_solution.reshape(1, R, B)
 
 
 def solution(mesh):

time: 99.1 us -> 94.3 us (0.952)
  local copies, waits for them, and re-layouts: 4.38 us -> 0.03 us
  waiting for transfers between devices: 3.03 us -> 1.52 us
  Pallas kernels: 9.32 us -> 10.4 us
    unnamed x16 -> x10, local copies, waits for them, and re-layouts: 4.38 us -> 0.03 us
    ppermute x1, waiting for transfers between devices: 1.51 us -> 0.01 us  [shards(): other = lax.ppermute(mine, 'c', swap)]
    pallas_call x2 -> x3, Pallas kernels: 7.21 us -> 8.33 us  [the longest x1 4.18 us: shards(): call(link_kernel, (shape((leaves, NC, RH, B), BF16), shape(face, F32), sh...]
  transfers between devices with their start and end apart: 2 -> 2, of which waited for: 2 -> 1; matrix products, arithmetic and copies ran while one was open for 0% -> 0% of each run, Pallas kernels for 0% -> 2%
where the time goes in v2:
time: 94.3 us; the launch traced here: 94 us
  blocking collectives  65 us (69%)
  starting transfers between devices  16.2 us (17%)
  Pallas kernels  10.4 us (11%)
  waiting for transfers between devices  1.52 us (2%)
    all_to_all x1, blocking collectives, shards(): parts = lax.all_to_all(sums, 'z', 0, 0, tiled=True)  24.6 us
    all_to_all x1, blocking collectives, shards(): planes = lax.all_to_all(solved, 'z', 0, 0, tiled=True)  14.4 us
    all_to_all x1, blocking collectives, shards(): parts = lax.all_to_all(pairs, FACE, 0, 0, tiled=True)  13.6 us
    all_to_all x1, blocking collectives, shards(): mine = lax.all_to_all(picked, FACE, 0, 0, tiled=True)  12.4 us
    ppermute x1, starting transfers between devices, shards(): part = lax.ppermute(send, 'c', swap)  9.05 us
    ppermute x1, starting transfers between devices, shards(): other = lax.ppermute(mine, 'c', swap)  7.17 us
    pallas_call x1, Pallas kernels, shards(): call(link_kernel, (shape((leaves, NC, RH, B), BF16), shape(face, F32), sh...  4.18 us
    pallas_call x1, Pallas kernels, shards(): call(other_kernel, (shape((leaves, NC, RH, B), BF16), shape((1, NC, RH, B...  2.4 us
  transfers between devices with their start and end apart: 2, of which 1 were waited for; matrix products, arithmetic and copies ran while one was open for 0% of the time, Pallas kernels for 2%

profile of v2, /device:TPU:1, one launch (start us, length us, event | category | flops | bytes accessed | tf_op | source)
XLA Modules:
  0.0 94.0 jit_solution(4267840915076246163)
XLA Ops:
  0.6 0.1 pad_add_fusion.at_ref
  0.7 4.2 %shard_map.77 = (bf16[2,2,32,256]{3,2,1,0:T(8,128)(2,1)S(1)}, f32[16,64,256]{2,1,0:T(8,128)S(1)}, bf16[16,64,256]{2,1,0:T(8,128)(2,1)S(1)}) custom-call(s32[4]{0:T(128)S(1)} %pad_add_fusion.at_ref, s32[2,12]{1,0:T(2,128)} %links_ref.3, bf16[2,64,256]{2,1,0:T(8,128)(2,1)} %rhs_hbm.1, bf16[2,256,256]{2,1,0:T(8,128)(2,1)} %inverse_ref.5, ...), custom_call_target="tpu_custom_call" | custom-call | tf_op jit(solution)/shard_map/pallas_call | solution.py:184
  4.9 0.0 copy-start
  4.9 0.0 copy-start.1
  4.9 0.0 copy-start.4
  4.9 9.1 %collective-permute-start = (bf16[16,64,256]{2,1,0:T(8,128)(2,1)S(1)}, bf16[16,64,256]{2,1,0:T(8,128)(2,1)S(1)}, u32[]{:S(2)}, u32[]{:S(2)}) collective-permute-start(bf16[16,64,256]{2,1,0:T(8,128)(2,1)S(1)} %get-tuple-element.10), channel_id=1, source_target_pairs={{0,1},{1,0},{2,3},{3,2},{4,5},{5,4},{6,7},{7,6},{8,9},{9,8},{10,11... | collective-permute-start | bytes 1572872 | tf_op jit(solution)/shard_map/ppermute | solution.py:197
  14.0 1.5 %collective-permute-done.part_ref = bf16[16,64,256]{2,1,0:T(8,128)(2,1)S(1)} collective-permute-done((bf16[16,64,256]{2,1,0:T(8,128)(2,1)S(1)}, bf16[16,64,256]{2,1,0:T(8,128)(2,1)S(1)}, u32[]{:S(2)}, u32[]{:S(2)}) %collective-permute-start) | collective-permute-done | bytes 524320 | tf_op jit(solution)/shard_map/ppermute | solution.py:197
  15.5 0.1 shard_map.78
  15.6 13.6 %all_to_all.20.parts_ref = bf16[16,64,256]{2,1,0:T(8,128)(2,1)S(1)} all-to-all(bf16[16,64,256]{2,1,0:T(8,128)(2,1)S(1)} %shard_map.78), channel_id=1, replica_groups=mesh['z'=16,'y'=4,'x'=4,'c'=2] {'y','x'}, dimensions={0} | all-to-all | bytes 1048576 | tf_op jit(solution)/shard_map/all_to_all | solution.py:199
  29.2 0.6 shard_map.79
  29.8 24.6 %all_to_all.21.parts_ref = bf16[16,16,128]{2,1,0:T(8,128)(2,1)S(1)} all-to-all(bf16[16,16,128]{2,1,0:T(8,128)(2,1)S(1)} %shard_map.79), channel_id=1, replica_groups=mesh['z'=16,'y'=4,'x'=4,'c'=2] {'z'}, dimensions={0} | all-to-all | bytes 131072 | tf_op jit(solution)/shard_map/all_to_all | solution.py:201
  54.4 0.0 copy-done.2
  54.4 0.0 copy-done.3
  54.4 0.8 shard_map.80
  55.2 14.4 %all_to_all.22.planes_ref = bf16[16,16,128]{2,1,0:T(8,128)(2,1)S(1)} all-to-all(bf16[16,16,128]{2,1,0:T(8,128)(2,1)S(1)} %shard_map.80), channel_id=1, replica_groups=mesh['z'=16,'y'=4,'x'=4,'c'=2] {'z'}, dimensions={0} | all-to-all | bytes 131072 | tf_op jit(solution)/shard_map/all_to_all | solution.py:205
  69.6 0.6 shard_map.81
  70.2 12.4 %all_to_all.23.parts_ref = bf16[16,64,256]{2,1,0:T(8,128)(2,1)S(1)} all-to-all(bf16[16,64,256]{2,1,0:T(8,128)(2,1)S(1)} %shard_map.81), channel_id=1, replica_groups=mesh['z'=16,'y'=4,'x'=4,'c'=2] {'y','x'}, dimensions={0} | all-to-all | bytes 1048576 | tf_op jit(solution)/shard_map/all_to_all | solution.py:207
  82.6 7.2 %collective-permute-start.1 = (bf16[16,64,256]{2,1,0:T(8,128)(2,1)S(1)}, bf16[16,64,256]{2,1,0:T(8,128)(2,1)S(1)}, u32[]{:S(2)}, u32[]{:S(2)}) collective-permute-start(bf16[16,64,256]{2,1,0:T(8,128)(2,1)S(1)} %all_to_all.23.parts_ref), channel_id=1, source_target_pairs={{0,1},{1,0},{2,3},{3,2},{4,5},{5,4},{6,7},{7,6},{8,9},{9,8},{10,11... | collective-permute-start | bytes 1572872 | tf_op jit(solution)/shard_map/ppermute | solution.py:208
  89.8 0.0 copy-done
  89.8 0.0 copy-done.1
  89.8 0.0 copy-done.4
  89.8 1.8 %shard_map.82 = (bf16[2,32,256]{2,1,0:T(8,128)(2,1)S(1)}, bf16[32,256]{1,0:T(8,128)(2,1)S(1)}) custom-call(s32[4]{0:T(128)S(1)} %pad_add_fusion.at_ref, s32[2,12]{1,0:T(2,128)S(1)} %copy-done.4, bf16[16,64,256]{2,1,0:T(8,128)(2,1)S(1)} %all_to_all.23.parts_ref, bf16[2,3072,256]{2,1,0:T(8,128)(2,1)S(1)} %bitcast.9, ...), custom_call_target="tpu_custom_call" | custom-call | tf_op jit(solution)/shard_map/pallas_call | solution.py:211
  91.6 0.0 collective-permute-done.1.parts_ref
  91.6 2.4 %shard_map.83 = (bf16[2,2,32,256]{3,2,1,0:T(8,128)(2,1)}, bf16[1,2,32,256]{3,2,1,0:T(8,128)(2,1)}) custom-call(s32[4]{0:T(128)S(1)} %pad_add_fusion.at_ref, s32[2,12]{1,0:T(2,128)S(1)} %copy-done.4, bf16[16,64,256]{2,1,0:T(8,128)(2,1)S(1)} %collective-permute-done.1.parts_ref, bf16[2,3072,256]{2,1,0:T(8,128)(2,1)S(1)} %bitcast.10, ...), custom_call_target="tpu_custom_call" | custom-call | tf_op jit(solution)/shard_map/pallas_call | solution.py:214
  (2 shorter events, 0.0 us)
Async XLA Ops:
  0.7 53.7 %copy-start.2 = (bf16[1,256,256]{2,1,0:T(8,128)(2,1)S(1)}, bf16[1,256,256]{2,1,0:T(8,128)(2,1)}, u32[]{:S(2)}) copy-start(bf16[1,256,256]{2,1,0:T(8,128)(2,1)} %inverse_ref.3) | copy-start | bytes 393220
  0.7 53.7 %copy-start.3 = (bf16[1,64,256]{2,1,0:T(8,128)(2,1)S(1)}, bf16[1,64,256]{2,1,0:T(8,128)(2,1)}, u32[]{:S(2)}) copy-start(bf16[1,64,256]{2,1,0:T(8,128)(2,1)} %rhs_ref.1) | copy-start | bytes 98308
  4.9 84.9 %copy-start = (bf16[2,12,256,256]{3,2,1,0:T(8,128)(2,1)S(1)}, bf16[2,12,256,256]{3,2,1,0:T(8,128)(2,1)}, u32[]{:S(2)}) copy-start(bf16[2,12,256,256]{3,2,1,0:T(8,128)(2,1)} %param.8) | copy-start | bytes 9437188
  4.9 84.9 %copy-start.1 = (bf16[2,256,256]{2,1,0:T(8,128)(2,1)S(1)}, bf16[2,256,256]{2,1,0:T(8,128)(2,1)}, u32[]{:S(2)}) copy-start(bf16[2,256,256]{2,1,0:T(8,128)(2,1)} %inverse_ref.5) | copy-start | bytes 786436
  4.9 84.9 %copy-start.4 = (s32[2,12]{1,0:T(2,128)S(1)}, s32[2,12]{1,0:T(2,128)}, u32[]{:S(2)}) copy-start(s32[2,12]{1,0:T(2,128)} %links_ref.3) | copy-start | bytes 292
  4.9 10.6 %collective-permute-start = (bf16[16,64,256]{2,1,0:T(8,128)(2,1)S(1)}, bf16[16,64,256]{2,1,0:T(8,128)(2,1)S(1)}, u32[]{:S(2)}, u32[]{:S(2)}) collective-permute-start(bf16[16,64,256]{2,1,0:T(8,128)(2,1)S(1)} %get-tuple-element.10), channel_id=1, source_target_pairs={{0,1},{1,0},{2,3},{3,2},{4,5},{5,4},{6,7},{7,6},{8,9},{9,8},{10,11... | collective-permute-start | bytes 1572872 | tf_op jit(solution)/shard_map/ppermute | solution.py:197
  82.6 9.0 %collective-permute-start.1 = (bf16[16,64,256]{2,1,0:T(8,128)(2,1)S(1)}, bf16[16,64,256]{2,1,0:T(8,128)(2,1)S(1)}, u32[]{:S(2)}, u32[]{:S(2)}) collective-permute-start(bf16[16,64,256]{2,1,0:T(8,128)(2,1)S(1)} %all_to_all.23.parts_ref), channel_id=1, source_target_pairs={{0,1},{1,0},{2,3},{3,2},{4,5},{5,4},{6,7},{7,6},{8,9},{9,8},{10,11... | collective-permute-start | bytes 1572872 | tf_op jit(solution)/shard_map/ppermute | solution.py:208

commit v3 on v2

v3 whole, which is shorter than its diff:
```python
import jax
import jax.numpy as jnp
from jax import lax
from jax.experimental import pallas as pl
from jax.experimental.pallas import tpu as pltpu
from jax.sharding import Mesh
from jax.sharding import PartitionSpec as P

NZ, NY, NX, NC = 16, 4, 4, 2
FACE = ("y", "x")
NFACE = NY * NX
NEAR = (-2, -1, 0, 1, 2)
OWN, EDGE, FAR = 2, 5, 6
NSLOT = 7
R, B = 64, 256
RP = R // (NX * NC)
RH = R // NC
LANES = 128
CHUNKS = 3

F32, BF16 = jnp.float32, jnp.bfloat16
VMEM = pl.BlockSpec(memory_space=pltpu.VMEM)
HBM = pl.BlockSpec(memory_space=pltpu.HBM)
PARAMS = pltpu.CompilerParams(vmem_limit_bytes=32 * 1024 * 1024)


def dot_nt(a, b):
    return lax.dot_general(a, b, (((1,), (1,)), ((), ())), preferred_element_type=F32)


def dot_nn(a, b):
    return lax.dot_general(a, b, (((1,), (0,)), ((), ())), preferred_element_type=F32)


def slot_of(link, z):
    step = (link // NY - z - NEAR[0] + NZ) % NZ
    plane_slot = jnp.where(step <= EDGE, step, jnp.where(step == NZ - 1, EDGE, FAR))
    return (link % NY) * NSLOT + plane_slot


def plane_of(step, z):
    return (z + step + NZ) % NZ


def rows_of(x, c):
    return pl.ds(pl.multiple_of((c * NX + x) * RP, RP), RP)


def fold(rows):
    return jnp.concatenate([rows[..., :LANES], rows[..., LANES:]], axis=-2)


def unfold(tile):
    return jnp.concatenate([tile[..., :RP, :], tile[..., RP:, :]], axis=-1)


def link_kernel(links_hbm, rhs_hbm, inverse_hbm, lower_hbm, forward_ref, keep_ref, send_ref,
                links_ref, rhs_ref, inverse_ref, lower_ref, terms_ref, sems):
    leaves, links = links_ref.shape
    per = leaves * links // CHUNKS
    copies = [
        pltpu.make_async_copy(links_hbm, links_ref, sems.at[CHUNKS]),
        pltpu.make_async_copy(rhs_hbm, rhs_ref, sems.at[CHUNKS + 1]),
        pltpu.make_async_copy(inverse_hbm, inverse_ref, sems.at[CHUNKS + 2]),
    ] + [
        pltpu.make_async_copy(lower_hbm.at[pl.ds(n * per, per)], lower_ref.at[pl.ds(n * per, per)], sems.at[n])
        for n in range(CHUNKS)
    ]
    for copy in copies:
        copy.start()
    small, blocks = copies[1:3], copies[3:]
    z, c = lax.axis_index("z"), lax.axis_index("c")
    terms_ref[...] = jnp.zeros_like(terms_ref)
    for copy in small:
        copy.wait()
    for i in range(leaves):
        forward_ref[i] = dot_nt(rhs_ref[i], inverse_ref[i]).astype(BF16).reshape(NC, RH, B)
    copies[0].wait()
    for i in range(leaves):
        forward = forward_ref[i].reshape(R, B)
        for k in range(links):
            n = i * links + k
            if n % per == 0:
                blocks[n // per].wait()
            terms_ref[slot_of(links_ref[i, k], z)] = dot_nt(forward, lower_ref[n])
    for y in range(NY):
        for x in range(NX):
            slots = slice(y * NSLOT, (y + 1) * NSLOT)
            mine = fold(terms_ref[slots, rows_of(x, c), :])
            keep_ref[y * NX + x] = mine.reshape(NSLOT * 2 * RP, LANES)
            other = fold(terms_ref[slots, rows_of(x, 1 - c), :])
            send_ref[y * NX + x] = other.reshape(NSLOT * 2 * RP, LANES).astype(BF16)


def pair_kernel(keep_ref, part_ref, out_ref):
    out_ref[...] = (keep_ref[...] + part_ref[...].astype(F32)).astype(BF16)


def face_kernel(parts_ref, out_ref):
    z, y = lax.axis_index("z"), lax.axis_index("y")
    rows = []
    for w in range(NY):
        total = parts_ref[w * NX].astype(F32)
        for x in range(1, NX):
            total = total + parts_ref[w * NX + x].astype(F32)
        rows.append(total.reshape(NSLOT, 2 * RP, LANES))
    total = rows[0] + rows[1] + rows[2] + rows[3]
    below = rows[0][EDGE]
    for w in range(1, NY):
        below = below + jnp.where(w <= y, rows[w][EDGE], 0.0)
    above = jnp.zeros_like(below)
    for w in range(1, NY):
        above = above + jnp.where(w > y, rows[w][EDGE], 0.0)
    out_ref[...] = jnp.zeros_like(out_ref)
    for slot, step in enumerate(NEAR):
        out_ref[plane_of(step, z)] = total[slot].astype(BF16)
    out_ref[plane_of(-3, z)] = below.astype(BF16)
    out_ref[plane_of(3, z)] = above.astype(BF16)
    out_ref[plane_of(NZ // 2, z)] = total[FAR].astype(BF16)


def solve_kernel(parts_ref, rhs_ref, inverse_ref, out_ref, rhs32_ref):
    rhs32_ref[...] = rhs_ref[0].astype(F32)
    sums = parts_ref[0].astype(F32)
    for n in range(1, NZ):
        sums = sums + parts_ref[n].astype(F32)
    right_side = (rhs32_ref[rows_of(lax.axis_index("x"), lax.axis_index("c")), :] - unfold(sums)).astype(BF16)
    middle = dot_nt(right_side, inverse_ref[0]).astype(BF16)
    solved = dot_nn(middle, inverse_ref[0])
    out_ref[...] = jnp.broadcast_to(fold(solved).astype(BF16)[None], out_ref.shape)


def pick_kernel(planes_ref, out_ref):
    z, y = lax.axis_index("z"), lax.axis_index("y")
    near = [planes_ref[plane_of(step, z)] for step in NEAR]
    below, above, far = (planes_ref[plane_of(step, z)] for step in (-3, 3, NZ // 2))
    for w in range(NY):
        edge = jnp.where(w <= y, below.astype(F32), above.astype(F32)).astype(BF16)
        picked = jnp.concatenate(near + [edge, far], axis=0)
        for x in range(NX):
            out_ref[w * NX + x] = picked


def back_half(links_hbm, parts_ref, lower_ref, forward_ref, inverse_ref, links_ref, seps_ref, rows_ref, sem, half):
    leaves, links = links_ref.shape
    z, y = lax.axis_index("z"), lax.axis_index("y")
    copy = pltpu.make_async_copy(links_hbm, links_ref, sem)
    copy.start()
    for w in range(NY):
        for x in range(NX):
            part = parts_ref[w * NX + x].astype(F32).reshape(NSLOT, 2 * RP, LANES)
            seps_ref[w * NSLOT:(w + 1) * NSLOT, x * RP:(x + 1) * RP, :] = unfold(part)
    copy.wait()
    solved = []
    for i in range(leaves):
        for k in range(links):
            rows_ref[:, k * B:(k + 1) * B] = seps_ref[slot_of(links_ref[i, k], z)].astype(BF16)
        back_terms = dot_nn(rows_ref[...], lower_ref[i])
        remainder = (forward_ref[i, half].astype(F32) - back_terms).astype(BF16)
        solved.append(dot_nn(remainder, inverse_ref[i]).astype(BF16))
    return solved, seps_ref[y * NSLOT + OWN].astype(BF16)


def mine_kernel(links_hbm, parts_ref, lower_ref, forward_ref, inverse_ref, leaf_ref, sep_ref, *scratch):
    c = lax.axis_index("c")
    solved, sep = back_half(links_hbm, parts_ref, lower_ref, forward_ref, inverse_ref, *scratch, c)
    for i, rows in enumerate(solved):
        leaf_ref[i] = rows
    sep_ref[...] = sep


def other_kernel(links_hbm, parts_ref, lower_ref, forward_ref, inverse_ref, leaf_half_ref, sep_half_ref,
                 leaf_ref, sep_ref, *scratch):
    c = lax.axis_index("c")
    solved, sep = back_half(links_hbm, parts_ref, lower_ref, forward_ref, inverse_ref, *scratch, 1 - c)
    for i, rows in enumerate(solved):
        leaf_ref[i, c] = leaf_half_ref[i]
        leaf_ref[i, 1 - c] = rows
    sep_ref[0, c] = sep_half_ref[...]
    sep_ref[0, 1 - c] = sep


def stay(array):
    return pltpu.with_memory_space_constraint(array, pltpu.HBM)


def call(kernel, outs, in_specs, scratch=()):
    many = isinstance(outs, tuple)
    return pl.pallas_call(
        kernel,
        out_shape=outs,
        in_specs=in_specs,
        out_specs=tuple(VMEM for _ in outs) if many else VMEM,
        scratch_shapes=scratch,
        compiler_params=PARAMS,
    )


def shards(leaf_rhs, leaf_inverse, leaf_lower, leaf_links, sep_rhs, sep_inverse):
    leaves, links = leaf_links.shape
    shape = jax.ShapeDtypeStruct
    swap = [(0, 1), (1, 0)]
    face = (NFACE, NSLOT * 2 * RP, LANES)
    column = (NZ, 2 * RP, LANES)
    forward, keep, send = call(
        link_kernel,
        (shape((leaves, NC, RH, B), BF16), shape(face, F32), shape(face, BF16)),
        [HBM, HBM, HBM, HBM],
        (
            pltpu.SMEM((leaves, links), jnp.int32),
            pltpu.VMEM((leaves, R, B), BF16),
            pltpu.VMEM((leaves, B, B), BF16),
            pltpu.VMEM((leaves * links, B, B), BF16),
            pltpu.VMEM((NY * NSLOT, R, B), F32),
            pltpu.SemaphoreType.DMA((CHUNKS + 3,)),
        ),
    )(*map(stay, (leaf_links, leaf_rhs, leaf_inverse, leaf_lower.reshape(leaves * links, B, B))))
    part = lax.ppermute(send, "c", swap)
    pairs = call(pair_kernel, shape(face, BF16), [VMEM, VMEM])(keep, part)
    parts = lax.all_to_all(pairs, FACE, 0, 0, tiled=True)
    sums = call(face_kernel, shape(column, BF16), [VMEM])(parts)
    parts = lax.all_to_all(sums, "z", 0, 0, tiled=True)
    solved = call(
        solve_kernel, shape(column, BF16), [VMEM, VMEM, VMEM], (pltpu.VMEM((R, B), F32),)
    )(parts, sep_rhs, sep_inverse)
    planes = lax.all_to_all(solved, "z", 0, 0, tiled=True)
    picked = call(pick_kernel, shape(face, BF16), [VMEM])(planes)
    mine = lax.all_to_all(picked, FACE, 0, 0, tiled=True)
    other = lax.ppermute(mine, "c", swap)
    lower = leaf_lower.reshape(leaves, links * B, B)
    scratch = (
        pltpu.SMEM((leaves, links), jnp.int32),
        pltpu.VMEM((NY * NSLOT, RH, B), F32),
        pltpu.VMEM((RH, links * B), BF16),
        pltpu.SemaphoreType.DMA(()),
    )
    halves = call(
        mine_kernel, (shape((leaves, RH, B), BF16), shape((RH, B), BF16)), [HBM] + [VMEM] * 4, scratch
    )(stay(leaf_links), mine, lower, forward, leaf_inverse)
    leaf_solution, sep_solution = call(
        other_kernel,
        (shape((leaves, NC, RH, B), BF16), shape((1, NC, RH, B), BF16)),
        [HBM] + [VMEM] * 6,
        scratch,
    )(stay(leaf_links), other, lower, forward, leaf_inverse, *halves)
    return leaf_solution.reshape(leaves, R, B), sep_solution.reshape(1, R, B)


def solution(mesh):
    grid = Mesh(mesh.devices.reshape(NZ, NY, NX, NC), ("z", "y", "x", "c"))
    every, row = ("z", "y", "x", "c"), ("z", "y")
    return jax.shard_map(
        shards,
        mesh=grid,
        in_specs=(P(every), P(every), P(every), P(every), P(row), P(row)),
        out_specs=(P(every), P(row)),
        check_vma=False,
    )
```

time: 94.3 us -> 90.3 us (0.958)
  Pallas kernels: 10.4 us -> 7.73 us
  blocking collectives: 65 us -> 63.7 us
    pallas_call x3, Pallas kernels: 2.02 us -> 0.4 us  [the longest x1 0.27 us: shards(): call(solve_kernel, shape(column, BF16), [VMEM, VMEM, VMEM], (pltpu.VMEM((...]
    pallas_call x1, Pallas kernels: 4.18 us -> 2.89 us  [shards(): call(link_kernel, (shape((leaves, NC, RH, B), BF16), shape(face, F32), sh...]
where the time goes in v3:
time: 90.3 us; the launch traced here: 90 us
  blocking collectives  63.7 us (71%)
  starting transfers between devices  16.4 us (18%)
  Pallas kernels  7.73 us (9%)
  waiting for transfers between devices  1.42 us (2%)
    all_to_all x1, blocking collectives, shards(): parts = lax.all_to_all(sums, 'z', 0, 0, tiled=True)  24.5 us
    all_to_all x1, blocking collectives, shards(): planes = lax.all_to_all(solved, 'z', 0, 0, tiled=True)  14.4 us
    all_to_all x1, blocking collectives, shards(): parts = lax.all_to_all(pairs, FACE, 0, 0, tiled=True)  12.9 us
    all_to_all x1, blocking collectives, shards(): mine = lax.all_to_all(picked, FACE, 0, 0, tiled=True)  11.9 us
    ppermute x1, starting transfers between devices, shards(): part = lax.ppermute(send, 'c', swap)  9.05 us
    ppermute x1, starting transfers between devices, shards(): other = lax.ppermute(mine, 'c', swap)  7.31 us
    pallas_call x1, Pallas kernels, shards(): call(link_kernel, (shape((leaves, NC, RH, B), BF16), shape(face, F32), sh...  2.89 us
    pallas_call x1, Pallas kernels, shards(): call(other_kernel, (shape((leaves, NC, RH, B), BF16), shape((1, NC, RH, B...  2.49 us
  transfers between devices with their start and end apart: 2, of which 1 were waited for; matrix products, arithmetic and copies ran while one was open for 0% of the time, Pallas kernels for 2%

profile of v3, /device:TPU:1, one launch (start us, length us, event | category | flops | bytes accessed | tf_op | source)
XLA Modules:
  0.0 90.0 jit_solution(10478819128337532538)
XLA Ops:
  0.6 0.0 copy-start.2
  0.6 0.0 copy-start.3
  0.6 2.9 %shard_map.77 = (bf16[2,2,32,256]{3,2,1,0:T(8,128)(2,1)S(1)}, f32[16,112,128]{2,1,0:T(8,128)S(1)}, bf16[16,112,128]{2,1,0:T(8,128)(2,1)S(1)}) custom-call(s32[2,12]{1,0:T(2,128)} %links_hbm.5, bf16[2,64,256]{2,1,0:T(8,128)(2,1)} %rhs_hbm.1, bf16[2,256,256]{2,1,0:T(8,128)(2,1)} %inverse_ref.5, bf16[24,256,256]{2,1,0:T(8,128)(2,1)} %bitcast.4), custom_call_target="tpu_custom_call" | custom-call | tf_op jit(solution)/shard_map/pallas_call | solution.py:205
  3.5 0.0 copy-start
  3.6 0.0 copy-start.1
  3.6 9.1 %collective-permute-start = (bf16[16,112,128]{2,1,0:T(8,128)(2,1)S(1)}, bf16[16,112,128]{2,1,0:T(8,128)(2,1)S(1)}, u32[]{:S(2)}, u32[]{:S(2)}) collective-permute-start(bf16[16,112,128]{2,1,0:T(8,128)(2,1)S(1)} %get-tuple-element.10), channel_id=1, source_target_pairs={{0,1},{1,0},{2,3},{3,2},{4,5},{5,4},{6,7},{7,6},{8,9},{9,8},{10,11... | collective-permute-start | bytes 1376264 | tf_op jit(solution)/shard_map/ppermute | solution.py:218
  12.6 1.4 %collective-permute-done.part_ref = bf16[16,112,128]{2,1,0:T(8,128)(2,1)S(1)} collective-permute-done((bf16[16,112,128]{2,1,0:T(8,128)(2,1)S(1)}, bf16[16,112,128]{2,1,0:T(8,128)(2,1)S(1)}, u32[]{:S(2)}, u32[]{:S(2)}) %collective-permute-start) | collective-permute-done | bytes 458784 | tf_op jit(solution)/shard_map/ppermute | solution.py:218
  14.1 0.1 shard_map.78
  14.1 12.9 %all_to_all.20.parts_ref = bf16[16,112,128]{2,1,0:T(8,128)(2,1)S(1)} all-to-all(bf16[16,112,128]{2,1,0:T(8,128)(2,1)S(1)} %shard_map.78), channel_id=1, replica_groups=mesh['z'=16,'y'=4,'x'=4,'c'=2] {'y','x'}, dimensions={0} | all-to-all | bytes 917504 | tf_op jit(solution)/shard_map/all_to_all | solution.py:220
  27.0 0.1 shard_map.79
  27.1 24.5 %all_to_all.21.parts_ref = bf16[16,16,128]{2,1,0:T(8,128)(2,1)S(1)} all-to-all(bf16[16,16,128]{2,1,0:T(8,128)(2,1)S(1)} %shard_map.79), channel_id=1, replica_groups=mesh['z'=16,'y'=4,'x'=4,'c'=2] {'z'}, dimensions={0} | all-to-all | bytes 131072 | tf_op jit(solution)/shard_map/all_to_all | solution.py:222
  51.6 0.0 copy-done.2
  51.6 0.0 copy-done.3
  51.6 0.3 shard_map.80
  51.9 14.4 %all_to_all.22.planes_ref = bf16[16,16,128]{2,1,0:T(8,128)(2,1)S(1)} all-to-all(bf16[16,16,128]{2,1,0:T(8,128)(2,1)S(1)} %shard_map.80), channel_id=1, replica_groups=mesh['z'=16,'y'=4,'x'=4,'c'=2] {'z'}, dimensions={0} | all-to-all | bytes 131072 | tf_op jit(solution)/shard_map/all_to_all | solution.py:226
  66.3 0.1 shard_map.81
  66.4 11.9 %all_to_all.23.parts_ref = bf16[16,112,128]{2,1,0:T(8,128)(2,1)S(1)} all-to-all(bf16[16,112,128]{2,1,0:T(8,128)(2,1)S(1)} %shard_map.81), channel_id=1, replica_groups=mesh['z'=16,'y'=4,'x'=4,'c'=2] {'y','x'}, dimensions={0} | all-to-all | bytes 917504 | tf_op jit(solution)/shard_map/all_to_all | solution.py:228
  78.2 7.3 %collective-permute-start.1 = (bf16[16,112,128]{2,1,0:T(8,128)(2,1)S(1)}, bf16[16,112,128]{2,1,0:T(8,128)(2,1)S(1)}, u32[]{:S(2)}, u32[]{:S(2)}) collective-permute-start(bf16[16,112,128]{2,1,0:T(8,128)(2,1)S(1)} %all_to_all.23.parts_ref), channel_id=1, source_target_pairs={{0,1},{1,0},{2,3},{3,2},{4,5},{5,4},{6,7},{7,6},{8,9},{9,8},{10,11... | collective-permute-start | bytes 1376264 | tf_op jit(solution)/shard_map/ppermute | solution.py:229
  85.6 0.0 copy-done
  85.6 0.0 copy-done.1
  85.6 1.9 %shard_map.82 = (bf16[2,32,256]{2,1,0:T(8,128)(2,1)S(1)}, bf16[32,256]{1,0:T(8,128)(2,1)S(1)}) custom-call(s32[2,12]{1,0:T(2,128)} %links_hbm.5, bf16[16,112,128]{2,1,0:T(8,128)(2,1)S(1)} %all_to_all.23.parts_ref, bf16[2,3072,256]{2,1,0:T(8,128)(2,1)S(1)} %bitcast.5, bf16[2,2,32,256]{3,2,1,0:T(8,128)(2,1)S(1)} %get-tuple-element.11.forward_ref, ...), custom_call_target="tpu_custom_call" | custom-call | tf_op jit(solution)/shard_map/pallas_call | solution.py:237
  87.5 0.0 collective-permute-done.1.parts_ref
  87.5 2.5 %shard_map.83 = (bf16[2,2,32,256]{3,2,1,0:T(8,128)(2,1)}, bf16[1,2,32,256]{3,2,1,0:T(8,128)(2,1)}) custom-call(s32[2,12]{1,0:T(2,128)} %links_hbm.5, bf16[16,112,128]{2,1,0:T(8,128)(2,1)S(1)} %collective-permute-done.1.parts_ref, bf16[2,3072,256]{2,1,0:T(8,128)(2,1)S(1)} %bitcast.6, bf16[2,2,32,256]{3,2,1,0:T(8,128)(2,1)S(1)} %get-tuple-element.11.forward_ref, ...), custom_call_target="tpu_custom_call" | custom-call | tf_op jit(solution)/shard_map/pallas_call | solution.py:240
Async XLA Ops:
  0.6 51.0 %copy-start.2 = (bf16[1,256,256]{2,1,0:T(8,128)(2,1)S(1)}, bf16[1,256,256]{2,1,0:T(8,128)(2,1)}, u32[]{:S(2)}) copy-start(bf16[1,256,256]{2,1,0:T(8,128)(2,1)} %inverse_ref.3) | copy-start | bytes 393220
  0.6 51.0 %copy-start.3 = (bf16[1,64,256]{2,1,0:T(8,128)(2,1)S(1)}, bf16[1,64,256]{2,1,0:T(8,128)(2,1)}, u32[]{:S(2)}) copy-start(bf16[1,64,256]{2,1,0:T(8,128)(2,1)} %rhs_ref.1) | copy-start | bytes 98308
  3.5 82.0 %copy-start = (bf16[2,12,256,256]{3,2,1,0:T(8,128)(2,1)S(1)}, bf16[2,12,256,256]{3,2,1,0:T(8,128)(2,1)}, u32[]{:S(2)}) copy-start(bf16[2,12,256,256]{3,2,1,0:T(8,128)(2,1)} %param.8) | copy-start | bytes 9437188
  3.6 82.0 %copy-start.1 = (bf16[2,256,256]{2,1,0:T(8,128)(2,1)S(1)}, bf16[2,256,256]{2,1,0:T(8,128)(2,1)}, u32[]{:S(2)}) copy-start(bf16[2,256,256]{2,1,0:T(8,128)(2,1)} %inverse_ref.5) | copy-start | bytes 786436
  3.6 10.5 %collective-permute-start = (bf16[16,112,128]{2,1,0:T(8,128)(2,1)S(1)}, bf16[16,112,128]{2,1,0:T(8,128)(2,1)S(1)}, u32[]{:S(2)}, u32[]{:S(2)}) collective-permute-start(bf16[16,112,128]{2,1,0:T(8,128)(2,1)S(1)} %get-tuple-element.10), channel_id=1, source_target_pairs={{0,1},{1,0},{2,3},{3,2},{4,5},{5,4},{6,7},{7,6},{8,9},{9,8},{10,11... | collective-permute-start | bytes 1376264 | tf_op jit(solution)/shard_map/ppermute | solution.py:218
  78.2 9.2 %collective-permute-start.1 = (bf16[16,112,128]{2,1,0:T(8,128)(2,1)S(1)}, bf16[16,112,128]{2,1,0:T(8,128)(2,1)S(1)}, u32[]{:S(2)}, u32[]{:S(2)}) collective-permute-start(bf16[16,112,128]{2,1,0:T(8,128)(2,1)S(1)} %all_to_all.23.parts_ref), channel_id=1, source_target_pairs={{0,1},{1,0},{2,3},{3,2},{4,5},{5,4},{6,7},{7,6},{8,9},{9,8},{10,11... | collective-permute-start | bytes 1376264 | tf_op jit(solution)/shard_map/ppermute | solution.py:229

commit v4 on v3

--- a/solution.py
+++ b/solution.py
@@ -14,7 +14,6 @@
 NSLOT = 7
 R, B = 64, 256
 RP = R // (NX * NC)
-RH = R // NC
 LANES = 128
 CHUNKS = 3
 
@@ -74,10 +73,10 @@
     for copy in small:
         copy.wait()
     for i in range(leaves):
-        forward_ref[i] = dot_nt(rhs_ref[i], inverse_ref[i]).astype(BF16).reshape(NC, RH, B)
+        forward_ref[i] = dot_nt(rhs_ref[i], inverse_ref[i]).astype(BF16)
     copies[0].wait()
     for i in range(leaves):
-        forward = forward_ref[i].reshape(R, B)
+        forward = forward_ref[i]
         for k in range(links):
             n = i * links + k
             if n % per == 0:
@@ -92,8 +91,8 @@
             send_ref[y * NX + x] = other.reshape(NSLOT * 2 * RP, LANES).astype(BF16)
 
 
-def pair_kernel(keep_ref, part_ref, out_ref):
-    out_ref[...] = (keep_ref[...] + part_ref[...].astype(F32)).astype(BF16)
+def pair_kernel(keep_ref, sent_ref, out_ref):
+    out_ref[...] = (keep_ref[...] + sent_ref[1 - lax.axis_index("c")].astype(F32)).astype(BF16)
 
 
 def face_kernel(parts_ref, out_ref):
@@ -141,43 +140,24 @@
             out_ref[w * NX + x] = picked
 
 
-def back_half(links_hbm, parts_ref, lower_ref, forward_ref, inverse_ref, links_ref, seps_ref, rows_ref, sem, half):
+def back_kernel(links_vmem, parts_ref, lower_ref, forward_ref, inverse_ref, leaf_ref, sep_ref,
+                links_ref, seps_ref, sem):
     leaves, links = links_ref.shape
+    copy = pltpu.make_async_copy(links_vmem, links_ref, sem)
+    copy.start()
     z, y = lax.axis_index("z"), lax.axis_index("y")
-    copy = pltpu.make_async_copy(links_hbm, links_ref, sem)
-    copy.start()
     for w in range(NY):
-        for x in range(NX):
-            part = parts_ref[w * NX + x].astype(F32).reshape(NSLOT, 2 * RP, LANES)
-            seps_ref[w * NSLOT:(w + 1) * NSLOT, x * RP:(x + 1) * RP, :] = unfold(part)
+        for r in range(NC * NX):
+            part = parts_ref[r // NX, w * NX + r % NX].astype(F32).reshape(NSLOT, 2 * RP, LANES)
+            seps_ref[w * NSLOT:(w + 1) * NSLOT, r * RP:(r + 1) * RP, :] = unfold(part)
+    sep_ref[0] = seps_ref[y * NSLOT + OWN].astype(BF16)
     copy.wait()
-    solved = []
     for i in range(leaves):
+        back_terms = jnp.zeros((R, B), F32)
         for k in range(links):
-            rows_ref[:, k * B:(k + 1) * B] = seps_ref[slot_of(links_ref[i, k], z)].astype(BF16)
-        back_terms = dot_nn(rows_ref[...], lower_ref[i])
-        remainder = (forward_ref[i, half].astype(F32) - back_terms).astype(BF16)
-        solved.append(dot_nn(remainder, inverse_ref[i]).astype(BF16))
-    return solved, seps_ref[y * NSLOT + OWN].astype(BF16)
-
-
-def mine_kernel(links_hbm, parts_ref, lower_ref, forward_ref, inverse_ref, leaf_ref, sep_ref, *scratch):
-    c = lax.axis_index("c")
-    solved, sep = back_half(links_hbm, parts_ref, lower_ref, forward_ref, inverse_ref, *scratch, c)
-    for i, rows in enumerate(solved):
-        leaf_ref[i] = rows
-    sep_ref[...] = sep
-
-
-def other_kernel(links_hbm, parts_ref, lower_ref, forward_ref, inverse_ref, leaf_half_ref, sep_half_ref,
-                 leaf_ref, sep_ref, *scratch):
-    c = lax.axis_index("c")
-    solved, sep = back_half(links_hbm, parts_ref, lower_ref, forward_ref, inverse_ref, *scratch, 1 - c)
-    for i, rows in enumerate(solved):
-        leaf_ref[i, c] = leaf_half_ref[i]
-        leaf_ref[i, 1 - c] = rows
-    sep_ref[0, c] = sep_half_ref[...]
-    sep_ref[0, 1 - c] = sep
+            back_terms += dot_nn(seps_ref[slot_of(links_ref[i, k], z)].astype(BF16), lower_ref[i * links + k])
+        remainder = (forward_ref[i].astype(F32) - back_terms).astype(BF16)
+        leaf_ref[i] = dot_nn(remainder, inverse_ref[i]).astype(BF16)
 
 
 def stay(array):
@@ -199,12 +179,12 @@
 def shards(leaf_rhs, leaf_inverse, leaf_lower, leaf_links, sep_rhs, sep_inverse):
     leaves, links = leaf_links.shape
     shape = jax.ShapeDtypeStruct
-    swap = [(0, 1), (1, 0)]
     face = (NFACE, NSLOT * 2 * RP, LANES)
     column = (NZ, 2 * RP, LANES)
+    lower = leaf_lower.reshape(leaves * links, B, B)
     forward, keep, send = call(
         link_kernel,
-        (shape((leaves, NC, RH, B), BF16), shape(face, F32), shape(face, BF16)),
+        (shape((leaves, R, B), BF16), shape(face, F32), shape(face, BF16)),
         [HBM, HBM, HBM, HBM],
         (
             pltpu.SMEM((leaves, links), jnp.int32),
@@ -214,9 +194,9 @@
             pltpu.VMEM((NY * NSLOT, R, B), F32),
             pltpu.SemaphoreType.DMA((CHUNKS + 3,)),
         ),
-    )(*map(stay, (leaf_links, leaf_rhs, leaf_inverse, leaf_lower.reshape(leaves * links, B, B))))
-    part = lax.ppermute(send, "c", swap)
-    pairs = call(pair_kernel, shape(face, BF16), [VMEM, VMEM])(keep, part)
+    )(*map(stay, (leaf_links, leaf_rhs, leaf_inverse, lower)))
+    sent = lax.all_gather(send, "c")
+    pairs = call(pair_kernel, shape(face, BF16), [VMEM, VMEM])(keep, sent)
     parts = lax.all_to_all(pairs, FACE, 0, 0, tiled=True)
     sums = call(face_kernel, shape(column, BF16), [VMEM])(parts)
     parts = lax.all_to_all(sums, "z", 0, 0, tiled=True)
@@ -225,25 +205,18 @@
     )(parts, sep_rhs, sep_inverse)
     planes = lax.all_to_all(solved, "z", 0, 0, tiled=True)
     picked = call(pick_kernel, shape(face, BF16), [VMEM])(planes)
-    mine = lax.all_to_all(picked, FACE, 0, 0, tiled=True)
-    other = lax.ppermute(mine, "c", swap)
-    lower = leaf_lower.reshape(leaves, links * B, B)
-    scratch = (
-        pltpu.SMEM((leaves, links), jnp.int32),
-        pltpu.VMEM((NY * NSLOT, RH, B), F32),
-        pltpu.VMEM((RH, links * B), BF16),
-        pltpu.SemaphoreType.DMA(()),
-    )
-    halves = call(
-        mine_kernel, (shape((leaves, RH, B), BF16), shape((RH, B), BF16)), [HBM] + [VMEM] * 4, scratch
-    )(stay(leaf_links), mine, lower, forward, leaf_inverse)
-    leaf_solution, sep_solution = call(
-        other_kernel,
-        (shape((leaves, NC, RH, B), BF16), shape((1, NC, RH, B), BF16)),
-        [HBM] + [VMEM] * 6,
-        scratch,
-    )(stay(leaf_links), other, lower, forward, leaf_inverse, *halves)
-    return leaf_solution.reshape(leaves, R, B), sep_solution.reshape(1, R, B)
+    half = lax.all_to_all(picked, FACE, 0, 0, tiled=True)
+    parts = lax.all_gather(half, "c")
+    return call(
+        back_kernel,
+        (shape((leaves, R, B), BF16), shape((1, R, B), BF16)),
+        [VMEM] * 5,
+        (
+            pltpu.SMEM((leaves, links), jnp.int32),
+            pltpu.VMEM((NY * NSLOT, R, B), F32),
+            pltpu.SemaphoreType.DMA(()),
+        ),
+    )(leaf_links, parts, lower, forward, leaf_inverse)
 
 
 def solution(mesh):

time: 90.3 us -> 87.3 us (0.967)
  blocking collectives: 63.7 us -> 80.6 us
  starting transfers between devices: 16.4 us -> 0 us
  Pallas kernels: 7.73 us -> 5.78 us
  waiting for transfers between devices: 1.42 us -> 0 us
    all_gather x0 -> x2, blocking collectives: none -> 16.6 us  [the longest x1 9.1 us: shards(): sent = lax.all_gather(send, 'c')]
    ppermute x2 -> x0, starting transfers between devices: 16.4 us -> none  [the longest x1 9.05 us: shards(): part = lax.ppermute(send, 'c', swap)]
    pallas_call x4 -> x3, Pallas kernels: 7.33 us -> 5.38 us  [the longest x1 2.86 us: shards(): call(link_kernel, (shape((leaves, R, B), BF16), shape(face, F32), shape(f...]
    ppermute x2 -> x0, waiting for transfers between devices: 1.42 us -> none  [the longest x1 1.42 us: shards(): part = lax.ppermute(send, 'c', swap)]
  transfers between devices with their start and end apart: 2 -> 0, of which waited for: 1 -> 0; matrix products, arithmetic and copies ran while one was open for 0% -> 0% of each run, Pallas kernels for 2% -> 0%
where the time goes in v4:
time: 87.3 us; the launch traced here: 87 us
  blocking collectives  80.6 us (92%)
  Pallas kernels  5.78 us (7%)
    all_to_all x1, blocking collectives, shards(): parts = lax.all_to_all(sums, 'z', 0, 0, tiled=True)  24.5 us
    all_to_all x1, blocking collectives, shards(): planes = lax.all_to_all(solved, 'z', 0, 0, tiled=True)  14.4 us
    all_to_all x1, blocking collectives, shards(): parts = lax.all_to_all(pairs, FACE, 0, 0, tiled=True)  13.2 us
    all_to_all x1, blocking collectives, shards(): half = lax.all_to_all(picked, FACE, 0, 0, tiled=True)  11.9 us
    all_gather x1, blocking collectives, shards(): sent = lax.all_gather(send, 'c')  9.1 us
    all_gather x1, blocking collectives, shards(): parts = lax.all_gather(half, 'c')  7.49 us
    pallas_call x1, Pallas kernels, shards(): call(link_kernel, (shape((leaves, R, B), BF16), shape(face, F32), shape(f...  2.86 us
    pallas_call x1, Pallas kernels, shards(): call(back_kernel, (shape((leaves, R, B), BF16), shape((1, R, B), BF16)),...  2.45 us

profile of v4, /device:TPU:1, one launch (start us, length us, event | category | flops | bytes accessed | tf_op | source)
XLA Modules:
  0.0 87.0 jit_solution(1591197674996191822)
XLA Ops:
  0.6 2.9 %shard_map.77 = (bf16[2,64,256]{2,1,0:T(8,128)(2,1)S(1)}, f32[16,112,128]{2,1,0:T(8,128)S(1)}, bf16[16,112,128]{2,1,0:T(8,128)(2,1)S(1)}) custom-call(s32[2,12]{1,0:T(2,128)} %links_vmem.1, bf16[2,64,256]{2,1,0:T(8,128)(2,1)} %rhs_hbm.1, bf16[2,256,256]{2,1,0:T(8,128)(2,1)} %inverse_ref.3, bf16[24,256,256]{2,1,0:T(8,128)(2,1)} %bitcast.3), custom_call_target="tpu_custom_call" | custom-call | tf_op jit(solution)/shard_map/pallas_call | solution.py:185
  3.5 0.0 copy-start.2
  3.5 0.0 copy-start.3
  3.5 9.1 %all-gather = bf16[32,112,128]{2,1,0:T(8,128)(2,1)S(1)} all-gather(bf16[16,112,128]{2,1,0:T(8,128)(2,1)S(1)} %get-tuple-element.6), channel_id=2, replica_groups=mesh['z'=16,'y'=4,'x'=4,'c'=2] {'c'}, dimensions={0}, use_global_device_ids=true | all-gather | bytes 1376256 | tf_op jit(solution)/shard_map/all_gather | solution.py:198
  12.6 0.0 copy-start
  12.6 0.0 copy-start.1
  12.6 0.0 copy-start.4
  12.6 0.1 shard_map.78
  12.7 13.2 %all_to_all.20.parts_ref = bf16[16,112,128]{2,1,0:T(8,128)(2,1)S(1)} all-to-all(bf16[16,112,128]{2,1,0:T(8,128)(2,1)S(1)} %shard_map.78), channel_id=1, replica_groups=mesh['z'=16,'y'=4,'x'=4,'c'=2] {'y','x'}, dimensions={0} | all-to-all | bytes 917504 | tf_op jit(solution)/shard_map/all_to_all | solution.py:200
  25.9 0.1 shard_map.79
  26.0 24.5 %all_to_all.21.parts_ref = bf16[16,16,128]{2,1,0:T(8,128)(2,1)S(1)} all-to-all(bf16[16,16,128]{2,1,0:T(8,128)(2,1)S(1)} %shard_map.79), channel_id=1, replica_groups=mesh['z'=16,'y'=4,'x'=4,'c'=2] {'z'}, dimensions={0} | all-to-all | bytes 131072 | tf_op jit(solution)/shard_map/all_to_all | solution.py:202
  50.5 0.0 copy-done.2
  50.5 0.0 copy-done.3
  50.5 0.3 shard_map.80
  50.7 14.4 %all_to_all.22.planes_ref = bf16[16,16,128]{2,1,0:T(8,128)(2,1)S(1)} all-to-all(bf16[16,16,128]{2,1,0:T(8,128)(2,1)S(1)} %shard_map.80), channel_id=1, replica_groups=mesh['z'=16,'y'=4,'x'=4,'c'=2] {'z'}, dimensions={0} | all-to-all | bytes 131072 | tf_op jit(solution)/shard_map/all_to_all | solution.py:206
  65.1 0.1 shard_map.81
  65.2 11.9 %all_to_all.23 = bf16[16,112,128]{2,1,0:T(8,128)(2,1)S(1)} all-to-all(bf16[16,112,128]{2,1,0:T(8,128)(2,1)S(1)} %shard_map.81), channel_id=1, replica_groups=mesh['z'=16,'y'=4,'x'=4,'c'=2] {'y','x'}, dimensions={0} | all-to-all | bytes 917504 | tf_op jit(solution)/shard_map/all_to_all | solution.py:208
  77.1 7.5 %all-gather.1 = bf16[32,112,128]{2,1,0:T(8,128)(2,1)S(1)} all-gather(bf16[16,112,128]{2,1,0:T(8,128)(2,1)S(1)} %all_to_all.23), channel_id=3, replica_groups=mesh['z'=16,'y'=4,'x'=4,'c'=2] {'c'}, dimensions={0}, use_global_device_ids=true | all-gather | bytes 1376256 | tf_op jit(solution)/shard_map/all_gather | solution.py:209
  84.6 0.0 copy-done
  84.6 0.0 copy-done.1
  84.6 0.0 copy-done.4
  84.6 2.4 %shard_map.82 = (bf16[2,64,256]{2,1,0:T(8,128)(2,1)}, bf16[1,64,256]{2,1,0:T(8,128)(2,1)}) custom-call(s32[2,12]{1,0:T(2,128)S(1)} %copy-done.4, bf16[2,16,112,128]{3,2,1,0:T(8,128)(2,1)S(1)} %bitcast.5, bf16[24,256,256]{2,1,0:T(8,128)(2,1)S(1)} %bitcast.4, bf16[2,64,256]{2,1,0:T(8,128)(2,1)S(1)} %get-tuple-element.7.forward_ref, ...), custom_call_target="tpu_custom_call" | custom-call | tf_op jit(solution)/shard_map/pallas_call | solution.py:210
Async XLA Ops:
  3.5 47.0 %copy-start.2 = (bf16[1,256,256]{2,1,0:T(8,128)(2,1)S(1)}, bf16[1,256,256]{2,1,0:T(8,128)(2,1)}, u32[]{:S(2)}) copy-start(bf16[1,256,256]{2,1,0:T(8,128)(2,1)} %inverse_ref.2) | copy-start | bytes 393220
  3.5 47.0 %copy-start.3 = (bf16[1,64,256]{2,1,0:T(8,128)(2,1)S(1)}, bf16[1,64,256]{2,1,0:T(8,128)(2,1)}, u32[]{:S(2)}) copy-start(bf16[1,64,256]{2,1,0:T(8,128)(2,1)} %rhs_ref.1) | copy-start | bytes 98308
  12.6 72.0 %copy-start = (bf16[2,12,256,256]{3,2,1,0:T(8,128)(2,1)S(1)}, bf16[2,12,256,256]{3,2,1,0:T(8,128)(2,1)}, u32[]{:S(2)}) copy-start(bf16[2,12,256,256]{3,2,1,0:T(8,128)(2,1)} %param.8) | copy-start | bytes 9437188
  12.6 72.0 %copy-start.1 = (bf16[2,256,256]{2,1,0:T(8,128)(2,1)S(1)}, bf16[2,256,256]{2,1,0:T(8,128)(2,1)}, u32[]{:S(2)}) copy-start(bf16[2,256,256]{2,1,0:T(8,128)(2,1)} %inverse_ref.3) | copy-start | bytes 786436
  12.6 72.0 %copy-start.4 = (s32[2,12]{1,0:T(2,128)S(1)}, s32[2,12]{1,0:T(2,128)}, u32[]{:S(2)}) copy-start(s32[2,12]{1,0:T(2,128)} %links_vmem.1) | copy-start | bytes 292

commit v5 on v4

--- a/solution.py
+++ b/solution.py
@@ -19,6 +19,7 @@
 
 F32, BF16 = jnp.float32, jnp.bfloat16
 VMEM = pl.BlockSpec(memory_space=pltpu.VMEM)
+SMEM = pl.BlockSpec(memory_space=pltpu.SMEM)
 HBM = pl.BlockSpec(memory_space=pltpu.HBM)
 PARAMS = pltpu.CompilerParams(vmem_limit_bytes=32 * 1024 * 1024)
 
@@ -53,7 +54,7 @@
     return jnp.concatenate([tile[..., :RP, :], tile[..., RP:, :]], axis=-1)
 
 
-def link_kernel(links_hbm, rhs_hbm, inverse_hbm, lower_hbm, forward_ref, keep_ref, send_ref,
+def link_kernel(links_hbm, rhs_hbm, inverse_hbm, lower_hbm, forward_ref, keep_ref, send_ref, slots_ref,
                 links_ref, rhs_ref, inverse_ref, lower_ref, terms_ref, sems):
     leaves, links = links_ref.shape
     per = leaves * links // CHUNKS
@@ -81,7 +82,9 @@
             n = i * links + k
             if n % per == 0:
                 blocks[n // per].wait()
-            terms_ref[slot_of(links_ref[i, k], z)] = dot_nt(forward, lower_ref[n])
+            slot = slot_of(links_ref[i, k], z)
+            slots_ref[i, k] = slot
+            terms_ref[slot] = dot_nt(forward, lower_ref[n])
     for y in range(NY):
         for x in range(NX):
             slots = slice(y * NSLOT, (y + 1) * NSLOT)
@@ -140,37 +143,34 @@
             out_ref[w * NX + x] = picked
 
 
-def back_kernel(links_vmem, parts_ref, lower_ref, forward_ref, inverse_ref, leaf_ref, sep_ref,
-                links_ref, seps_ref, sem):
-    leaves, links = links_ref.shape
-    copy = pltpu.make_async_copy(links_vmem, links_ref, sem)
-    copy.start()
-    z, y = lax.axis_index("z"), lax.axis_index("y")
+def back_kernel(slots_ref, parts_ref, lower_ref, forward_ref, inverse_ref, leaf_ref, sep_ref, seps_ref):
+    leaves, links = slots_ref.shape
+    y = lax.axis_index("y")
     for w in range(NY):
         for r in range(NC * NX):
             part = parts_ref[r // NX, w * NX + r % NX].astype(F32).reshape(NSLOT, 2 * RP, LANES)
             seps_ref[w * NSLOT:(w + 1) * NSLOT, r * RP:(r + 1) * RP, :] = unfold(part)
     sep_ref[0] = seps_ref[y * NSLOT + OWN].astype(BF16)
-    copy.wait()
+    remainders = []
     for i in range(leaves):
         back_terms = jnp.zeros((R, B), F32)
         for k in range(links):
-            back_terms += dot_nn(seps_ref[slot_of(links_ref[i, k], z)].astype(BF16), lower_ref[i * links + k])
-        remainder = (forward_ref[i].astype(F32) - back_terms).astype(BF16)
-        leaf_ref[i] = dot_nn(remainder, inverse_ref[i]).astype(BF16)
+            back_terms += dot_nn(seps_ref[slots_ref[i, k]].astype(BF16), lower_ref[i * links + k])
+        remainders.append((forward_ref[i].astype(F32) - back_terms).astype(BF16))
+    for i in range(leaves):
+        leaf_ref[i] = dot_nn(remainders[i], inverse_ref[i]).astype(BF16)
 
 
 def stay(array):
     return pltpu.with_memory_space_constraint(array, pltpu.HBM)
 
 
-def call(kernel, outs, in_specs, scratch=()):
-    many = isinstance(outs, tuple)
+def call(kernel, outs, in_specs, scratch=(), out_specs=VMEM):
     return pl.pallas_call(
         kernel,
         out_shape=outs,
         in_specs=in_specs,
-        out_specs=tuple(VMEM for _ in outs) if many else VMEM,
+        out_specs=out_specs,
         scratch_shapes=scratch,
         compiler_params=PARAMS,
     )
@@ -182,9 +182,9 @@
     face = (NFACE, NSLOT * 2 * RP, LANES)
     column = (NZ, 2 * RP, LANES)
     lower = leaf_lower.reshape(leaves * links, B, B)
-    forward, keep, send = call(
+    forward, keep, send, slots = call(
         link_kernel,
-        (shape((leaves, R, B), BF16), shape(face, F32), shape(face, BF16)),
+        (shape((leaves, R, B), BF16), shape(face, F32), shape(face, BF16), pltpu.SMEM((leaves, links), jnp.int32)),
         [HBM, HBM, HBM, HBM],
         (
             pltpu.SMEM((leaves, links), jnp.int32),
@@ -194,6 +194,7 @@
             pltpu.VMEM((NY * NSLOT, R, B), F32),
             pltpu.SemaphoreType.DMA((CHUNKS + 3,)),
         ),
+        (VMEM, VMEM, VMEM, SMEM),
     )(*map(stay, (leaf_links, leaf_rhs, leaf_inverse, lower)))
     sent = lax.all_gather(send, "c")
     pairs = call(pair_kernel, shape(face, BF16), [VMEM, VMEM])(keep, sent)
@@ -210,13 +211,10 @@
     return call(
         back_kernel,
         (shape((leaves, R, B), BF16), shape((1, R, B), BF16)),
-        [VMEM] * 5,
-        (
-            pltpu.SMEM((leaves, links), jnp.int32),
-            pltpu.VMEM((NY * NSLOT, R, B), F32),
-            pltpu.SemaphoreType.DMA(()),
-        ),
-    )(leaf_links, parts, lower, forward, leaf_inverse)
+        [SMEM] + [VMEM] * 4,
+        (pltpu.VMEM((NY * NSLOT, R, B), F32),),
+        (VMEM, VMEM),
+    )(slots, parts, lower, forward, leaf_inverse)
 
 
 def solution(mesh):

time: 87.3 us -> 86.3 us (0.989)
  Pallas kernels: 5.78 us -> 4.85 us
    pallas_call x1, Pallas kernels: 2.45 us -> 1.52 us  [shards(): call(back_kernel, (shape((leaves, R, B), BF16), shape((1, R, B), BF16)),...]
where the time goes in v5:
time: 86.3 us; the launch traced here: 86.1 us
  blocking collectives  80.5 us (93%)
  Pallas kernels  4.85 us (6%)
    all_to_all x1, blocking collectives, shards(): parts = lax.all_to_all(sums, 'z', 0, 0, tiled=True)  24.5 us
    all_to_all x1, blocking collectives, shards(): planes = lax.all_to_all(solved, 'z', 0, 0, tiled=True)  14.4 us
    all_to_all x1, blocking collectives, shards(): parts = lax.all_to_all(pairs, FACE, 0, 0, tiled=True)  13.2 us
    all_to_all x1, blocking collectives, shards(): half = lax.all_to_all(picked, FACE, 0, 0, tiled=True)  11.9 us
    all_gather x1, blocking collectives, shards(): sent = lax.all_gather(send, 'c')  9.1 us
    all_gather x1, blocking collectives, shards(): parts = lax.all_gather(half, 'c')  7.49 us
    pallas_call x1, Pallas kernels, shards(): call(link_kernel, (shape((leaves, R, B), BF16), shape(face, F32), shape(f...  2.86 us

profile of v5, /device:TPU:1, one launch (start us, length us, event | category | flops | bytes accessed | tf_op | source)
XLA Modules:
  0.0 86.1 jit_solution(13164604623628573505)
XLA Ops:
  0.6 2.9 %shard_map.77 = (bf16[2,64,256]{2,1,0:T(8,128)(2,1)S(1)}, f32[16,112,128]{2,1,0:T(8,128)S(1)}, bf16[16,112,128]{2,1,0:T(8,128)(2,1)S(1)}, s32[2,12]{1,0:T(2,128)S(4)}) custom-call(s32[2,12]{1,0:T(2,128)} %links_hbm.1, bf16[2,64,256]{2,1,0:T(8,128)(2,1)} %rhs_hbm.1, bf16[2,256,256]{2,1,0:T(8,128)(2,1)} %inverse_ref.3, bf16[24,256,256]{2,1,0:T(8,128)(2,1)} %bitcast.3), custom_call_target="tpu_custom_call" | custom-call | tf_op jit(solution)/shard_map/pallas_call | solution.py:185
  3.5 0.0 copy-start.2
  3.5 0.0 copy-start.3
  3.5 9.1 %all-gather = bf16[32,112,128]{2,1,0:T(8,128)(2,1)S(1)} all-gather(bf16[16,112,128]{2,1,0:T(8,128)(2,1)S(1)} %get-tuple-element.8), channel_id=2, replica_groups=mesh['z'=16,'y'=4,'x'=4,'c'=2] {'c'}, dimensions={0}, use_global_device_ids=true | all-gather | bytes 1376256 | tf_op jit(solution)/shard_map/all_gather | solution.py:199
  12.6 0.0 copy-start
  12.6 0.0 copy-start.1
  12.6 0.1 shard_map.78
  12.7 13.2 %all_to_all.20.parts_ref = bf16[16,112,128]{2,1,0:T(8,128)(2,1)S(1)} all-to-all(bf16[16,112,128]{2,1,0:T(8,128)(2,1)S(1)} %shard_map.78), channel_id=1, replica_groups=mesh['z'=16,'y'=4,'x'=4,'c'=2] {'y','x'}, dimensions={0} | all-to-all | bytes 917504 | tf_op jit(solution)/shard_map/all_to_all | solution.py:201
  25.9 0.1 shard_map.79
  25.9 24.5 %all_to_all.21.parts_ref = bf16[16,16,128]{2,1,0:T(8,128)(2,1)S(1)} all-to-all(bf16[16,16,128]{2,1,0:T(8,128)(2,1)S(1)} %shard_map.79), channel_id=1, replica_groups=mesh['z'=16,'y'=4,'x'=4,'c'=2] {'z'}, dimensions={0} | all-to-all | bytes 131072 | tf_op jit(solution)/shard_map/all_to_all | solution.py:203
  50.4 0.0 copy-done.2
  50.4 0.0 copy-done.3
  50.4 0.3 shard_map.80
  50.7 14.4 %all_to_all.22.planes_ref = bf16[16,16,128]{2,1,0:T(8,128)(2,1)S(1)} all-to-all(bf16[16,16,128]{2,1,0:T(8,128)(2,1)S(1)} %shard_map.80), channel_id=1, replica_groups=mesh['z'=16,'y'=4,'x'=4,'c'=2] {'z'}, dimensions={0} | all-to-all | bytes 131072 | tf_op jit(solution)/shard_map/all_to_all | solution.py:207
  65.1 0.1 shard_map.81
  65.2 11.9 %all_to_all.23 = bf16[16,112,128]{2,1,0:T(8,128)(2,1)S(1)} all-to-all(bf16[16,112,128]{2,1,0:T(8,128)(2,1)S(1)} %shard_map.81), channel_id=1, replica_groups=mesh['z'=16,'y'=4,'x'=4,'c'=2] {'y','x'}, dimensions={0} | all-to-all | bytes 917504 | tf_op jit(solution)/shard_map/all_to_all | solution.py:209
  77.1 7.5 %all-gather.1 = bf16[32,112,128]{2,1,0:T(8,128)(2,1)S(1)} all-gather(bf16[16,112,128]{2,1,0:T(8,128)(2,1)S(1)} %all_to_all.23), channel_id=3, replica_groups=mesh['z'=16,'y'=4,'x'=4,'c'=2] {'c'}, dimensions={0}, use_global_device_ids=true | all-gather | bytes 1376256 | tf_op jit(solution)/shard_map/all_gather | solution.py:210
  84.6 0.0 copy-done
  84.6 0.0 copy-done.1
  84.6 1.5 %shard_map.82 = (bf16[2,64,256]{2,1,0:T(8,128)(2,1)}, bf16[1,64,256]{2,1,0:T(8,128)(2,1)}) custom-call(s32[2,12]{1,0:T(2,128)S(4)} %get-tuple-element.6.slots_ref, bf16[2,16,112,128]{3,2,1,0:T(8,128)(2,1)S(1)} %bitcast.5, bf16[24,256,256]{2,1,0:T(8,128)(2,1)S(1)} %bitcast.4, bf16[2,64,256]{2,1,0:T(8,128)(2,1)S(1)} %get-tuple-element.9.forward_ref, ...), custom_call_target="tpu_custom_call" | custom-call | tf_op jit(solution)/shard_map/pallas_call | solution.py:211
Async XLA Ops:
  3.5 47.0 %copy-start.2 = (bf16[1,256,256]{2,1,0:T(8,128)(2,1)S(1)}, bf16[1,256,256]{2,1,0:T(8,128)(2,1)}, u32[]{:S(2)}) copy-start(bf16[1,256,256]{2,1,0:T(8,128)(2,1)} %inverse_ref.2) | copy-start | bytes 393220
  3.5 46.9 %copy-start.3 = (bf16[1,64,256]{2,1,0:T(8,128)(2,1)S(1)}, bf16[1,64,256]{2,1,0:T(8,128)(2,1)}, u32[]{:S(2)}) copy-start(bf16[1,64,256]{2,1,0:T(8,128)(2,1)} %rhs_ref.1) | copy-start | bytes 98308
  12.6 71.9 %copy-start = (bf16[2,12,256,256]{3,2,1,0:T(8,128)(2,1)S(1)}, bf16[2,12,256,256]{3,2,1,0:T(8,128)(2,1)}, u32[]{:S(2)}) copy-start(bf16[2,12,256,256]{3,2,1,0:T(8,128)(2,1)} %param.8) | copy-start | bytes 9437188
  12.6 71.9 %copy-start.1 = (bf16[2,256,256]{2,1,0:T(8,128)(2,1)S(1)}, bf16[2,256,256]{2,1,0:T(8,128)(2,1)}, u32[]{:S(2)}) copy-start(bf16[2,256,256]{2,1,0:T(8,128)(2,1)} %inverse_ref.3) | copy-start | bytes 786436

commit v6 on v5

--- a/solution.py
+++ b/solution.py
@@ -9,6 +9,9 @@
 NZ, NY, NX, NC = 16, 4, 4, 2
 FACE = ("y", "x")
 NFACE = NY * NX
+FIRST_PLANE, FIRST_PLACE = 8, 2 * NX + 2
+PLANES = [[(FIRST_PLANE + n) % NZ for n in range(NZ)]]
+PLACES = [[(FIRST_PLACE + n) % NFACE for n in range(NFACE)]]
 NEAR = (-2, -1, 0, 1, 2)
 OWN, EDGE, FAR = 2, 5, 6
 NSLOT = 7
@@ -39,7 +42,11 @@
 
 
 def plane_of(step, z):
-    return (z + step + NZ) % NZ
+    return (z + step + 2 * NZ - FIRST_PLANE) % NZ
+
+
+def place_of(y, x):
+    return (y * NX + x + NFACE - FIRST_PLACE) % NFACE
 
 
 def rows_of(x, c):
@@ -89,9 +96,9 @@
         for x in range(NX):
             slots = slice(y * NSLOT, (y + 1) * NSLOT)
             mine = fold(terms_ref[slots, rows_of(x, c), :])
-            keep_ref[y * NX + x] = mine.reshape(NSLOT * 2 * RP, LANES)
+            keep_ref[place_of(y, x)] = mine.reshape(NSLOT * 2 * RP, LANES)
             other = fold(terms_ref[slots, rows_of(x, 1 - c), :])
-            send_ref[y * NX + x] = other.reshape(NSLOT * 2 * RP, LANES).astype(BF16)
+            send_ref[place_of(y, x)] = other.reshape(NSLOT * 2 * RP, LANES).astype(BF16)
 
 
 def pair_kernel(keep_ref, sent_ref, out_ref):
@@ -102,9 +109,9 @@
     z, y = lax.axis_index("z"), lax.axis_index("y")
     rows = []
     for w in range(NY):
-        total = parts_ref[w * NX].astype(F32)
+        total = parts_ref[place_of(w, 0)].astype(F32)
         for x in range(1, NX):
-            total = total + parts_ref[w * NX + x].astype(F32)
+            total = total + parts_ref[place_of(w, x)].astype(F32)
         rows.append(total.reshape(NSLOT, 2 * RP, LANES))
     total = rows[0] + rows[1] + rows[2] + rows[3]
     below = rows[0][EDGE]
@@ -140,7 +147,7 @@
         edge = jnp.where(w <= y, below.astype(F32), above.astype(F32)).astype(BF16)
         picked = jnp.concatenate(near + [edge, far], axis=0)
         for x in range(NX):
-            out_ref[w * NX + x] = picked
+            out_ref[place_of(w, x)] = picked
 
 
 def back_kernel(slots_ref, parts_ref, lower_ref, forward_ref, inverse_ref, leaf_ref, sep_ref, seps_ref):
@@ -148,7 +155,7 @@
     y = lax.axis_index("y")
     for w in range(NY):
         for r in range(NC * NX):
-            part = parts_ref[r // NX, w * NX + r % NX].astype(F32).reshape(NSLOT, 2 * RP, LANES)
+            part = parts_ref[r // NX, place_of(w, r % NX)].astype(F32).reshape(NSLOT, 2 * RP, LANES)
             seps_ref[w * NSLOT:(w + 1) * NSLOT, r * RP:(r + 1) * RP, :] = unfold(part)
     sep_ref[0] = seps_ref[y * NSLOT + OWN].astype(BF16)
     remainders = []
@@ -174,6 +181,10 @@
         scratch_shapes=scratch,
         compiler_params=PARAMS,
     )
+
+
+def exchange(blocks, axes, order):
+    return lax.all_to_all(blocks, axes, 0, 0, tiled=True, axis_index_groups=order)
 
 
 def shards(leaf_rhs, leaf_inverse, leaf_lower, leaf_links, sep_rhs, sep_inverse):
@@ -198,15 +209,15 @@
     )(*map(stay, (leaf_links, leaf_rhs, leaf_inverse, lower)))
     sent = lax.all_gather(send, "c")
     pairs = call(pair_kernel, shape(face, BF16), [VMEM, VMEM])(keep, sent)
-    parts = lax.all_to_all(pairs, FACE, 0, 0, tiled=True)
+    parts = exchange(pairs, FACE, PLACES)
     sums = call(face_kernel, shape(column, BF16), [VMEM])(parts)
-    parts = lax.all_to_all(sums, "z", 0, 0, tiled=True)
+    parts = exchange(sums, "z", PLANES)
     solved = call(
         solve_kernel, shape(column, BF16), [VMEM, VMEM, VMEM], (pltpu.VMEM((R, B), F32),)
     )(parts, sep_rhs, sep_inverse)
-    planes = lax.all_to_all(solved, "z", 0, 0, tiled=True)
+    planes = exchange(solved, "z", PLANES)
     picked = call(pick_kernel, shape(face, BF16), [VMEM])(planes)
-    half = lax.all_to_all(picked, FACE, 0, 0, tiled=True)
+    half = exchange(picked, FACE, PLACES)
     parts = lax.all_gather(half, "c")
     return call(
         back_kernel,

time: 86.3 us -> 77 us (0.89)
  blocking collectives: 80.5 us -> 71.2 us
    all_to_all x4, blocking collectives: 64 us -> 56.7 us  [exchange(): lax.all_to_all(blocks, axes, 0, 0, tiled=True, axis_index_groups=order)]
    all_gather x1, blocking collectives: 7.49 us -> 5.44 us  [shards(): parts = lax.all_gather(half, 'c')]
where the time goes in v6:
time: 77 us; the launch traced here: 76.7 us
  blocking collectives  71.2 us (92%)
  Pallas kernels  4.85 us (6%)
    all_to_all x4, blocking collectives, exchange(): lax.all_to_all(blocks, axes, 0, 0, tiled=True, axis_index_groups=order)  56.7 us
    all_gather x1, blocking collectives, shards(): sent = lax.all_gather(send, 'c')  9.1 us
    all_gather x1, blocking collectives, shards(): parts = lax.all_gather(half, 'c')  5.44 us
    pallas_call x1, Pallas kernels, shards(): call(link_kernel, (shape((leaves, R, B), BF16), shape(face, F32), shape(f...  2.86 us

profile of v6, /device:TPU:1, one launch (start us, length us, event | category | flops | bytes accessed | tf_op | source)
XLA Modules:
  0.0 76.7 jit_solution(967277222239817)
XLA Ops:
  0.6 2.9 %shard_map.77 = (bf16[2,64,256]{2,1,0:T(8,128)(2,1)S(1)}, f32[16,112,128]{2,1,0:T(8,128)S(1)}, bf16[16,112,128]{2,1,0:T(8,128)(2,1)S(1)}, s32[2,12]{1,0:T(2,128)S(4)}) custom-call(s32[2,12]{1,0:T(2,128)} %links_hbm.1, bf16[2,64,256]{2,1,0:T(8,128)(2,1)} %rhs_hbm.1, bf16[2,256,256]{2,1,0:T(8,128)(2,1)} %inverse_ref.3, bf16[24,256,256]{2,1,0:T(8,128)(2,1)} %bitcast.3), custom_call_target="tpu_custom_call" | custom-call | tf_op jit(solution)/shard_map/pallas_call | solution.py:196
  3.5 0.0 copy-start.2
  3.5 0.0 copy-start.3
  3.5 9.1 %all-gather = bf16[32,112,128]{2,1,0:T(8,128)(2,1)S(1)} all-gather(bf16[16,112,128]{2,1,0:T(8,128)(2,1)S(1)} %get-tuple-element.8), channel_id=2, replica_groups=mesh['z'=16,'y'=4,'x'=4,'c'=2] {'c'}, dimensions={0}, use_global_device_ids=true | all-gather | bytes 1376256 | tf_op jit(solution)/shard_map/all_gather | solution.py:210
  12.6 0.0 copy-start
  12.6 0.0 copy-start.1
  12.6 0.1 shard_map.78
  12.7 12.9 %all_to_all.20.parts_ref = bf16[16,112,128]{2,1,0:T(8,128)(2,1)S(1)} all-to-all(bf16[16,112,128]{2,1,0:T(8,128)(2,1)S(1)} %shard_map.78), channel_id=1, replica_groups={{20,22,24,26,28,30,0,2,4,6,8,10,12,14,16,18},{21,23,25,27,29,31,1,3,5,7..., dimensions={0} | all-to-all | bytes 917504 | tf_op jit(solution)/shard_map/all_to_all | solution.py:187
  25.6 0.1 shard_map.79
  25.6 17.5 %all_to_all.21.parts_ref = bf16[16,16,128]{2,1,0:T(8,128)(2,1)S(1)} all-to-all(bf16[16,16,128]{2,1,0:T(8,128)(2,1)S(1)} %shard_map.79), channel_id=1, replica_groups={{256,288,320,352,384,416,448,480,0,32,64,96,128,160,192,224},{257,289,3..., dimensions={0} | all-to-all | bytes 131072 | tf_op jit(solution)/shard_map/all_to_all | solution.py:187
  43.1 0.0 copy-done.2
  43.1 0.0 copy-done.3
  43.2 0.3 shard_map.80
  43.4 14.4 %all_to_all.22.planes_ref = bf16[16,16,128]{2,1,0:T(8,128)(2,1)S(1)} all-to-all(bf16[16,16,128]{2,1,0:T(8,128)(2,1)S(1)} %shard_map.80), channel_id=1, replica_groups={{256,288,320,352,384,416,448,480,0,32,64,96,128,160,192,224},{257,289,3..., dimensions={0} | all-to-all | bytes 131072 | tf_op jit(solution)/shard_map/all_to_all | solution.py:187
  57.8 0.1 shard_map.81
  57.9 11.9 %all_to_all.23 = bf16[16,112,128]{2,1,0:T(8,128)(2,1)S(1)} all-to-all(bf16[16,112,128]{2,1,0:T(8,128)(2,1)S(1)} %shard_map.81), channel_id=1, replica_groups={{20,22,24,26,28,30,0,2,4,6,8,10,12,14,16,18},{21,23,25,27,29,31,1,3,5,7..., dimensions={0} | all-to-all | bytes 917504 | tf_op jit(solution)/shard_map/all_to_all | solution.py:187
  69.8 5.4 %all-gather.1 = bf16[32,112,128]{2,1,0:T(8,128)(2,1)S(1)} all-gather(bf16[16,112,128]{2,1,0:T(8,128)(2,1)S(1)} %all_to_all.23), channel_id=3, replica_groups=mesh['z'=16,'y'=4,'x'=4,'c'=2] {'c'}, dimensions={0}, use_global_device_ids=true | all-gather | bytes 1376256 | tf_op jit(solution)/shard_map/all_gather | solution.py:221
  75.2 0.0 copy-done
  75.2 0.0 copy-done.1
  75.2 1.5 %shard_map.82 = (bf16[2,64,256]{2,1,0:T(8,128)(2,1)}, bf16[1,64,256]{2,1,0:T(8,128)(2,1)}) custom-call(s32[2,12]{1,0:T(2,128)S(4)} %get-tuple-element.6.slots_ref, bf16[2,16,112,128]{3,2,1,0:T(8,128)(2,1)S(1)} %bitcast.5, bf16[24,256,256]{2,1,0:T(8,128)(2,1)S(1)} %bitcast.4, bf16[2,64,256]{2,1,0:T(8,128)(2,1)S(1)} %get-tuple-element.9.forward_ref, ...), custom_call_target="tpu_custom_call" | custom-call | tf_op jit(solution)/shard_map/pallas_call | solution.py:222
Async XLA Ops:
  3.5 39.7 %copy-start.2 = (bf16[1,256,256]{2,1,0:T(8,128)(2,1)S(1)}, bf16[1,256,256]{2,1,0:T(8,128)(2,1)}, u32[]{:S(2)}) copy-start(bf16[1,256,256]{2,1,0:T(8,128)(2,1)} %inverse_ref.2) | copy-start | bytes 393220
  3.5 39.6 %copy-start.3 = (bf16[1,64,256]{2,1,0:T(8,128)(2,1)S(1)}, bf16[1,64,256]{2,1,0:T(8,128)(2,1)}, u32[]{:S(2)}) copy-start(bf16[1,64,256]{2,1,0:T(8,128)(2,1)} %rhs_ref.1) | copy-start | bytes 98308
  12.6 62.6 %copy-start = (bf16[2,12,256,256]{3,2,1,0:T(8,128)(2,1)S(1)}, bf16[2,12,256,256]{3,2,1,0:T(8,128)(2,1)}, u32[]{:S(2)}) copy-start(bf16[2,12,256,256]{3,2,1,0:T(8,128)(2,1)} %param.8) | copy-start | bytes 9437188
  12.6 62.6 %copy-start.1 = (bf16[2,256,256]{2,1,0:T(8,128)(2,1)S(1)}, bf16[2,256,256]{2,1,0:T(8,128)(2,1)}, u32[]{:S(2)}) copy-start(bf16[2,256,256]{2,1,0:T(8,128)(2,1)} %inverse_ref.3) | copy-start | bytes 786436

commit v7 on v5

--- a/solution.py
+++ b/solution.py
@@ -9,13 +9,14 @@
 NZ, NY, NX, NC = 16, 4, 4, 2
 FACE = ("y", "x")
 NFACE = NY * NX
+FIRST_PLANES, FIRST_PLACES = (8, 8), (10, 10)
 NEAR = (-2, -1, 0, 1, 2)
 OWN, EDGE, FAR = 2, 5, 6
 NSLOT = 7
 R, B = 64, 256
 RP = R // (NX * NC)
 LANES = 128
-CHUNKS = 3
+CHUNKS = 2
 
 F32, BF16 = jnp.float32, jnp.bfloat16
 VMEM = pl.BlockSpec(memory_space=pltpu.VMEM)
@@ -38,8 +39,12 @@
     return (link % NY) * NSLOT + plane_slot
 
 
-def plane_of(step, z):
-    return (z + step + NZ) % NZ
+def plane_of(step, z, turn):
+    return (z + step + 2 * NZ - FIRST_PLANES[turn]) % NZ
+
+
+def place_of(y, x, turn):
+    return (y * NX + x + NFACE - FIRST_PLACES[turn]) % NFACE
 
 
 def rows_of(x, c):
@@ -89,9 +94,9 @@
         for x in range(NX):
             slots = slice(y * NSLOT, (y + 1) * NSLOT)
             mine = fold(terms_ref[slots, rows_of(x, c), :])
-            keep_ref[y * NX + x] = mine.reshape(NSLOT * 2 * RP, LANES)
+            keep_ref[place_of(y, x, 0)] = mine.reshape(NSLOT * 2 * RP, LANES)
             other = fold(terms_ref[slots, rows_of(x, 1 - c), :])
-            send_ref[y * NX + x] = other.reshape(NSLOT * 2 * RP, LANES).astype(BF16)
+            send_ref[place_of(y, x, 0)] = other.reshape(NSLOT * 2 * RP, LANES).astype(BF16)
 
 
 def pair_kernel(keep_ref, sent_ref, out_ref):
@@ -102,9 +107,9 @@
     z, y = lax.axis_index("z"), lax.axis_index("y")
     rows = []
     for w in range(NY):
-        total = parts_ref[w * NX].astype(F32)
+        total = parts_ref[place_of(w, 0, 0)].astype(F32)
         for x in range(1, NX):
-            total = total + parts_ref[w * NX + x].astype(F32)
+            total = total + parts_ref[place_of(w, x, 0)].astype(F32)
         rows.append(total.reshape(NSLOT, 2 * RP, LANES))
     total = rows[0] + rows[1] + rows[2] + rows[3]
     below = rows[0][EDGE]
@@ -115,10 +120,10 @@
         above = above + jnp.where(w > y, rows[w][EDGE], 0.0)
     out_ref[...] = jnp.zeros_like(out_ref)
     for slot, step in enumerate(NEAR):
-        out_ref[plane_of(step, z)] = total[slot].astype(BF16)
-    out_ref[plane_of(-3, z)] = below.astype(BF16)
-    out_ref[plane_of(3, z)] = above.astype(BF16)
-    out_ref[plane_of(NZ // 2, z)] = total[FAR].astype(BF16)
+        out_ref[plane_of(step, z, 0)] = total[slot].astype(BF16)
+    out_ref[plane_of(-3, z, 0)] = below.astype(BF16)
+    out_ref[plane_of(3, z, 0)] = above.astype(BF16)
+    out_ref[plane_of(NZ // 2, z, 0)] = total[FAR].astype(BF16)
 
 
 def solve_kernel(parts_ref, rhs_ref, inverse_ref, out_ref, rhs32_ref):
@@ -134,28 +139,31 @@
 
 def pick_kernel(planes_ref, out_ref):
     z, y = lax.axis_index("z"), lax.axis_index("y")
-    near = [planes_ref[plane_of(step, z)] for step in NEAR]
-    below, above, far = (planes_ref[plane_of(step, z)] for step in (-3, 3, NZ // 2))
+    near = [planes_ref[plane_of(step, z, 1)] for step in NEAR]
+    below, above, far = (planes_ref[plane_of(step, z, 1)] for step in (-3, 3, NZ // 2))
     for w in range(NY):
         edge = jnp.where(w <= y, below.astype(F32), above.astype(F32)).astype(BF16)
         picked = jnp.concatenate(near + [edge, far], axis=0)
         for x in range(NX):
-            out_ref[w * NX + x] = picked
+            out_ref[place_of(w, x, 1)] = picked
 
 
 def back_kernel(slots_ref, parts_ref, lower_ref, forward_ref, inverse_ref, leaf_ref, sep_ref, seps_ref):
     leaves, links = slots_ref.shape
     y = lax.axis_index("y")
     for w in range(NY):
-        for r in range(NC * NX):
-            part = parts_ref[r // NX, w * NX + r % NX].astype(F32).reshape(NSLOT, 2 * RP, LANES)
-            seps_ref[w * NSLOT:(w + 1) * NSLOT, r * RP:(r + 1) * RP, :] = unfold(part)
-    sep_ref[0] = seps_ref[y * NSLOT + OWN].astype(BF16)
+        for r in range(0, NC * NX, 2):
+            pair = [
+                unfold(parts_ref[n // NX, place_of(w, n % NX, 1)].astype(F32).reshape(NSLOT, 2 * RP, LANES))
+                for n in (r, r + 1)
+            ]
+            seps_ref[w * NSLOT:(w + 1) * NSLOT, r * RP:(r + 2) * RP, :] = jnp.concatenate(pair, axis=1).astype(BF16)
+    sep_ref[0] = seps_ref[y * NSLOT + OWN]
     remainders = []
     for i in range(leaves):
         back_terms = jnp.zeros((R, B), F32)
         for k in range(links):
-            back_terms += dot_nn(seps_ref[slots_ref[i, k]].astype(BF16), lower_ref[i * links + k])
+            back_terms += dot_nn(seps_ref[slots_ref[i, k]], lower_ref[i * links + k])
         remainders.append((forward_ref[i].astype(F32) - back_terms).astype(BF16))
     for i in range(leaves):
         leaf_ref[i] = dot_nn(remainders[i], inverse_ref[i]).astype(BF16)
@@ -174,6 +182,12 @@
         scratch_shapes=scratch,
         compiler_params=PARAMS,
     )
+
+
+def exchange(blocks, axes, first):
+    count = blocks.shape[0]
+    order = [[(first + n) % count for n in range(count)]]
+    return lax.all_to_all(blocks, axes, 0, 0, tiled=True, axis_index_groups=order)
 
 
 def shards(leaf_rhs, leaf_inverse, leaf_lower, leaf_links, sep_rhs, sep_inverse):
@@ -198,21 +212,21 @@
     )(*map(stay, (leaf_links, leaf_rhs, leaf_inverse, lower)))
     sent = lax.all_gather(send, "c")
     pairs = call(pair_kernel, shape(face, BF16), [VMEM, VMEM])(keep, sent)
-    parts = lax.all_to_all(pairs, FACE, 0, 0, tiled=True)
+    parts = exchange(pairs, FACE, FIRST_PLACES[0])
     sums = call(face_kernel, shape(column, BF16), [VMEM])(parts)
-    parts = lax.all_to_all(sums, "z", 0, 0, tiled=True)
+    parts = exchange(sums, "z", FIRST_PLANES[0])
     solved = call(
         solve_kernel, shape(column, BF16), [VMEM, VMEM, VMEM], (pltpu.VMEM((R, B), F32),)
     )(parts, sep_rhs, sep_inverse)
-    planes = lax.all_to_all(solved, "z", 0, 0, tiled=True)
+    planes = exchange(solved, "z", FIRST_PLANES[1])
     picked = call(pick_kernel, shape(face, BF16), [VMEM])(planes)
-    half = lax.all_to_all(picked, FACE, 0, 0, tiled=True)
+    half = exchange(picked, FACE, FIRST_PLACES[1])
     parts = lax.all_gather(half, "c")
     return call(
         back_kernel,
         (shape((leaves, R, B), BF16), shape((1, R, B), BF16)),
         [SMEM] + [VMEM] * 4,
-        (pltpu.VMEM((NY * NSLOT, R, B), F32),),
+        (pltpu.VMEM((NY * NSLOT, R, B), BF16),),
         (VMEM, VMEM),
     )(slots, parts, lower, forward, leaf_inverse)
 

time: 86.3 us -> 77 us (0.89)
  blocking collectives: 80.5 us -> 71.2 us
    all_to_all x4, blocking collectives: 64 us -> 56.6 us  [exchange(): lax.all_to_all(blocks, axes, 0, 0, tiled=True, axis_index_groups=order)]
    all_gather x1, blocking collectives: 7.49 us -> 5.44 us  [shards(): parts = lax.all_gather(half, 'c')]
where the time goes in v7:
time: 77 us; the launch traced here: 76.7 us
  blocking collectives  71.2 us (92%)
  Pallas kernels  4.84 us (6%)
    all_to_all x4, blocking collectives, exchange(): lax.all_to_all(blocks, axes, 0, 0, tiled=True, axis_index_groups=order)  56.6 us
    all_gather x1, blocking collectives, shards(): sent = lax.all_gather(send, 'c')  9.1 us
    all_gather x1, blocking collectives, shards(): parts = lax.all_gather(half, 'c')  5.44 us
    pallas_call x1, Pallas kernels, shards(): call(link_kernel, (shape((leaves, R, B), BF16), shape(face, F32), shape(f...  2.9 us

profile of v7, /device:TPU:1, one launch (start us, length us, event | category | flops | bytes accessed | tf_op | source)
XLA Modules:
  0.0 76.7 jit_solution(12871496768876273361)
XLA Ops:
  0.6 2.9 %shard_map.77 = (bf16[2,64,256]{2,1,0:T(8,128)(2,1)S(1)}, f32[16,112,128]{2,1,0:T(8,128)S(1)}, bf16[16,112,128]{2,1,0:T(8,128)(2,1)S(1)}, s32[2,12]{1,0:T(2,128)S(4)}) custom-call(s32[2,12]{1,0:T(2,128)} %links_hbm.1, bf16[2,64,256]{2,1,0:T(8,128)(2,1)} %rhs_hbm.1, bf16[2,256,256]{2,1,0:T(8,128)(2,1)} %inverse_ref.3, bf16[24,256,256]{2,1,0:T(8,128)(2,1)} %bitcast.3), custom_call_target="tpu_custom_call" | custom-call | tf_op jit(solution)/shard_map/pallas_call | solution.py:199
  3.5 0.0 copy-start.2
  3.6 0.0 copy-start.3
  3.6 9.1 %all-gather = bf16[32,112,128]{2,1,0:T(8,128)(2,1)S(1)} all-gather(bf16[16,112,128]{2,1,0:T(8,128)(2,1)S(1)} %get-tuple-element.8), channel_id=2, replica_groups=mesh['z'=16,'y'=4,'x'=4,'c'=2] {'c'}, dimensions={0}, use_global_device_ids=true | all-gather | bytes 1376256 | tf_op jit(solution)/shard_map/all_gather | solution.py:213
  12.7 0.0 copy-start
  12.7 0.0 copy-start.1
  12.7 0.1 shard_map.78
  12.8 12.9 %all_to_all.20.parts_ref = bf16[16,112,128]{2,1,0:T(8,128)(2,1)S(1)} all-to-all(bf16[16,112,128]{2,1,0:T(8,128)(2,1)S(1)} %shard_map.78), channel_id=1, replica_groups={{20,22,24,26,28,30,0,2,4,6,8,10,12,14,16,18},{21,23,25,27,29,31,1,3,5,7..., dimensions={0} | all-to-all | bytes 917504 | tf_op jit(solution)/shard_map/all_to_all | solution.py:190
  25.6 0.1 shard_map.79
  25.7 17.5 %all_to_all.21.parts_ref = bf16[16,16,128]{2,1,0:T(8,128)(2,1)S(1)} all-to-all(bf16[16,16,128]{2,1,0:T(8,128)(2,1)S(1)} %shard_map.79), channel_id=1, replica_groups={{256,288,320,352,384,416,448,480,0,32,64,96,128,160,192,224},{257,289,3..., dimensions={0} | all-to-all | bytes 131072 | tf_op jit(solution)/shard_map/all_to_all | solution.py:190
  43.2 0.0 copy-done.2
  43.2 0.0 copy-done.3
  43.2 0.3 shard_map.80
  43.5 14.4 %all_to_all.22.planes_ref = bf16[16,16,128]{2,1,0:T(8,128)(2,1)S(1)} all-to-all(bf16[16,16,128]{2,1,0:T(8,128)(2,1)S(1)} %shard_map.80), channel_id=1, replica_groups={{256,288,320,352,384,416,448,480,0,32,64,96,128,160,192,224},{257,289,3..., dimensions={0} | all-to-all | bytes 131072 | tf_op jit(solution)/shard_map/all_to_all | solution.py:190
  57.9 0.1 shard_map.81
  58.0 11.9 %all_to_all.23 = bf16[16,112,128]{2,1,0:T(8,128)(2,1)S(1)} all-to-all(bf16[16,112,128]{2,1,0:T(8,128)(2,1)S(1)} %shard_map.81), channel_id=1, replica_groups={{20,22,24,26,28,30,0,2,4,6,8,10,12,14,16,18},{21,23,25,27,29,31,1,3,5,7..., dimensions={0} | all-to-all | bytes 917504 | tf_op jit(solution)/shard_map/all_to_all | solution.py:190
  69.8 5.4 %all-gather.1 = bf16[32,112,128]{2,1,0:T(8,128)(2,1)S(1)} all-gather(bf16[16,112,128]{2,1,0:T(8,128)(2,1)S(1)} %all_to_all.23), channel_id=3, replica_groups=mesh['z'=16,'y'=4,'x'=4,'c'=2] {'c'}, dimensions={0}, use_global_device_ids=true | all-gather | bytes 1376256 | tf_op jit(solution)/shard_map/all_gather | solution.py:224
  75.3 0.0 copy-done
  75.3 0.0 copy-done.1
  75.3 1.5 %shard_map.82 = (bf16[2,64,256]{2,1,0:T(8,128)(2,1)}, bf16[1,64,256]{2,1,0:T(8,128)(2,1)}) custom-call(s32[2,12]{1,0:T(2,128)S(4)} %get-tuple-element.6.slots_ref, bf16[2,16,112,128]{3,2,1,0:T(8,128)(2,1)S(1)} %bitcast.5, bf16[24,256,256]{2,1,0:T(8,128)(2,1)S(1)} %bitcast.4, bf16[2,64,256]{2,1,0:T(8,128)(2,1)S(1)} %get-tuple-element.9.forward_ref, ...), custom_call_target="tpu_custom_call" | custom-call | tf_op jit(solution)/shard_map/pallas_call | solution.py:225
Async XLA Ops:
  3.5 39.7 %copy-start.2 = (bf16[1,256,256]{2,1,0:T(8,128)(2,1)S(1)}, bf16[1,256,256]{2,1,0:T(8,128)(2,1)}, u32[]{:S(2)}) copy-start(bf16[1,256,256]{2,1,0:T(8,128)(2,1)} %inverse_ref.2) | copy-start | bytes 393220
  3.6 39.6 %copy-start.3 = (bf16[1,64,256]{2,1,0:T(8,128)(2,1)S(1)}, bf16[1,64,256]{2,1,0:T(8,128)(2,1)}, u32[]{:S(2)}) copy-start(bf16[1,64,256]{2,1,0:T(8,128)(2,1)} %rhs_ref.1) | copy-start | bytes 98308
  12.7 62.6 %copy-start = (bf16[2,12,256,256]{3,2,1,0:T(8,128)(2,1)S(1)}, bf16[2,12,256,256]{3,2,1,0:T(8,128)(2,1)}, u32[]{:S(2)}) copy-start(bf16[2,12,256,256]{3,2,1,0:T(8,128)(2,1)} %param.8) | copy-start | bytes 9437188
  12.7 62.6 %copy-start.1 = (bf16[2,256,256]{2,1,0:T(8,128)(2,1)S(1)}, bf16[2,256,256]{2,1,0:T(8,128)(2,1)}, u32[]{:S(2)}) copy-start(bf16[2,256,256]{2,1,0:T(8,128)(2,1)} %inverse_ref.3) | copy-start | bytes 786436

commit v8 on v7

--- a/solution.py
+++ b/solution.py
@@ -128,10 +128,10 @@
 
 def solve_kernel(parts_ref, rhs_ref, inverse_ref, out_ref, rhs32_ref):
     rhs32_ref[...] = rhs_ref[0].astype(F32)
-    sums = parts_ref[0].astype(F32)
-    for n in range(1, NZ):
-        sums = sums + parts_ref[n].astype(F32)
-    right_side = (rhs32_ref[rows_of(lax.axis_index("x"), lax.axis_index("c")), :] - unfold(sums)).astype(BF16)
+    sums = [parts_ref[n].astype(F32) for n in range(NZ)]
+    while len(sums) > 1:
+        sums = [a + b for a, b in zip(sums[::2], sums[1::2], strict=True)]
+    right_side = (rhs32_ref[rows_of(lax.axis_index("x"), lax.axis_index("c")), :] - unfold(sums[0])).astype(BF16)
     middle = dot_nt(right_side, inverse_ref[0]).astype(BF16)
     solved = dot_nn(middle, inverse_ref[0])
     out_ref[...] = jnp.broadcast_to(fold(solved).astype(BF16)[None], out_ref.shape)

time: 77 us -> 77 us (level)
  no operation moved by 1% of the time
where the time goes in v8:
time: 77 us; the launch traced here: 76.7 us
  blocking collectives  71.2 us (92%)
  Pallas kernels  4.84 us (6%)
    all_to_all x4, blocking collectives, exchange(): lax.all_to_all(blocks, axes, 0, 0, tiled=True, axis_index_groups=order)  56.7 us
    all_gather x1, blocking collectives, shards(): sent = lax.all_gather(send, 'c')  9.1 us
    all_gather x1, blocking collectives, shards(): parts = lax.all_gather(half, 'c')  5.44 us
    pallas_call x1, Pallas kernels, shards(): call(link_kernel, (shape((leaves, R, B), BF16), shape(face, F32), shape(f...  2.9 us

profile of v8, /device:TPU:1, one launch (start us, length us, event | category | flops | bytes accessed | tf_op | source)
XLA Modules:
  0.0 76.7 jit_solution(10616381442688341442)
XLA Ops:
  0.6 2.9 %shard_map.77 = (bf16[2,64,256]{2,1,0:T(8,128)(2,1)S(1)}, f32[16,112,128]{2,1,0:T(8,128)S(1)}, bf16[16,112,128]{2,1,0:T(8,128)(2,1)S(1)}, s32[2,12]{1,0:T(2,128)S(4)}) custom-call(s32[2,12]{1,0:T(2,128)} %links_hbm.1, bf16[2,64,256]{2,1,0:T(8,128)(2,1)} %rhs_hbm.1, bf16[2,256,256]{2,1,0:T(8,128)(2,1)} %inverse_ref.3, bf16[24,256,256]{2,1,0:T(8,128)(2,1)} %bitcast.3), custom_call_target="tpu_custom_call" | custom-call | tf_op jit(solution)/shard_map/pallas_call | solution.py:199
  3.5 0.0 copy-start.2
  3.6 0.0 copy-start.3
  3.6 9.1 %all-gather = bf16[32,112,128]{2,1,0:T(8,128)(2,1)S(1)} all-gather(bf16[16,112,128]{2,1,0:T(8,128)(2,1)S(1)} %get-tuple-element.8), channel_id=2, replica_groups=mesh['z'=16,'y'=4,'x'=4,'c'=2] {'c'}, dimensions={0}, use_global_device_ids=true | all-gather | bytes 1376256 | tf_op jit(solution)/shard_map/all_gather | solution.py:213
  12.7 0.0 copy-start
  12.7 0.0 copy-start.1
  12.7 0.1 shard_map.78
  12.8 12.9 %all_to_all.20.parts_ref = bf16[16,112,128]{2,1,0:T(8,128)(2,1)S(1)} all-to-all(bf16[16,112,128]{2,1,0:T(8,128)(2,1)S(1)} %shard_map.78), channel_id=1, replica_groups={{20,22,24,26,28,30,0,2,4,6,8,10,12,14,16,18},{21,23,25,27,29,31,1,3,5,7..., dimensions={0} | all-to-all | bytes 917504 | tf_op jit(solution)/shard_map/all_to_all | solution.py:190
  25.6 0.1 shard_map.79
  25.7 17.5 %all_to_all.21.parts_ref = bf16[16,16,128]{2,1,0:T(8,128)(2,1)S(1)} all-to-all(bf16[16,16,128]{2,1,0:T(8,128)(2,1)S(1)} %shard_map.79), channel_id=1, replica_groups={{256,288,320,352,384,416,448,480,0,32,64,96,128,160,192,224},{257,289,3..., dimensions={0} | all-to-all | bytes 131072 | tf_op jit(solution)/shard_map/all_to_all | solution.py:190
  43.2 0.0 copy-done.2
  43.2 0.0 copy-done.3
  43.2 0.3 shard_map.80
  43.5 14.4 %all_to_all.22.planes_ref = bf16[16,16,128]{2,1,0:T(8,128)(2,1)S(1)} all-to-all(bf16[16,16,128]{2,1,0:T(8,128)(2,1)S(1)} %shard_map.80), channel_id=1, replica_groups={{256,288,320,352,384,416,448,480,0,32,64,96,128,160,192,224},{257,289,3..., dimensions={0} | all-to-all | bytes 131072 | tf_op jit(solution)/shard_map/all_to_all | solution.py:190
  57.9 0.1 shard_map.81
  58.0 11.9 %all_to_all.23 = bf16[16,112,128]{2,1,0:T(8,128)(2,1)S(1)} all-to-all(bf16[16,112,128]{2,1,0:T(8,128)(2,1)S(1)} %shard_map.81), channel_id=1, replica_groups={{20,22,24,26,28,30,0,2,4,6,8,10,12,14,16,18},{21,23,25,27,29,31,1,3,5,7..., dimensions={0} | all-to-all | bytes 917504 | tf_op jit(solution)/shard_map/all_to_all | solution.py:190
  69.8 5.4 %all-gather.1 = bf16[32,112,128]{2,1,0:T(8,128)(2,1)S(1)} all-gather(bf16[16,112,128]{2,1,0:T(8,128)(2,1)S(1)} %all_to_all.23), channel_id=3, replica_groups=mesh['z'=16,'y'=4,'x'=4,'c'=2] {'c'}, dimensions={0}, use_global_device_ids=true | all-gather | bytes 1376256 | tf_op jit(solution)/shard_map/all_gather | solution.py:224
  75.3 0.0 copy-done
  75.3 0.0 copy-done.1
  75.3 1.5 %shard_map.82 = (bf16[2,64,256]{2,1,0:T(8,128)(2,1)}, bf16[1,64,256]{2,1,0:T(8,128)(2,1)}) custom-call(s32[2,12]{1,0:T(2,128)S(4)} %get-tuple-element.6.slots_ref, bf16[2,16,112,128]{3,2,1,0:T(8,128)(2,1)S(1)} %bitcast.5, bf16[24,256,256]{2,1,0:T(8,128)(2,1)S(1)} %bitcast.4, bf16[2,64,256]{2,1,0:T(8,128)(2,1)S(1)} %get-tuple-element.9.forward_ref, ...), custom_call_target="tpu_custom_call" | custom-call | tf_op jit(solution)/shard_map/pallas_call | solution.py:225
Async XLA Ops:
  3.5 39.7 %copy-start.2 = (bf16[1,256,256]{2,1,0:T(8,128)(2,1)S(1)}, bf16[1,256,256]{2,1,0:T(8,128)(2,1)}, u32[]{:S(2)}) copy-start(bf16[1,256,256]{2,1,0:T(8,128)(2,1)} %inverse_ref.2) | copy-start | bytes 393220
  3.6 39.6 %copy-start.3 = (bf16[1,64,256]{2,1,0:T(8,128)(2,1)S(1)}, bf16[1,64,256]{2,1,0:T(8,128)(2,1)}, u32[]{:S(2)}) copy-start(bf16[1,64,256]{2,1,0:T(8,128)(2,1)} %rhs_ref.1) | copy-start | bytes 98308
  12.7 62.6 %copy-start = (bf16[2,12,256,256]{3,2,1,0:T(8,128)(2,1)S(1)}, bf16[2,12,256,256]{3,2,1,0:T(8,128)(2,1)}, u32[]{:S(2)}) copy-start(bf16[2,12,256,256]{3,2,1,0:T(8,128)(2,1)} %param.8) | copy-start | bytes 9437188
  12.7 62.6 %copy-start.1 = (bf16[2,256,256]{2,1,0:T(8,128)(2,1)S(1)}, bf16[2,256,256]{2,1,0:T(8,128)(2,1)}, u32[]{:S(2)}) copy-start(bf16[2,256,256]{2,1,0:T(8,128)(2,1)} %inverse_ref.3) | copy-start | bytes 786436
